TPU v7x, 128 devices: a whole 4x4x4 slice. The times are simulated.
128 devices in a mesh: fsdp: 16 (over x, z_hi, core), tp: 8 (over z_lo, y).
Axes of the slice: x: 4, y: 4, z: 4 (z_hi: 2, z_lo: 2; z = z_hi * 2 + z_lo), core: 2. Of those that a mesh axis runs over, the one named last changes fastest.
Arguments:
- hidden_activations_saved: bfloat16 [2048, 26624], P('fsdp', 'tp'), may hold values from -6 to 6
- output_cotangent: bfloat16 [2048, 16384], P('tp', 'fsdp'), may hold values from -6 to 6
- frozen_down_matrix: bfloat16 [26624, 16384], P('tp', 'fsdp'), may hold values from -0.0390625 to 0.0390625
- adapter_input_maps: bfloat16 [16, 26624, 16], P('fsdp', 'tp'), may hold values from -0.078125 to 0.078125
- adapter_output_maps: bfloat16 [16, 16, 16384], P('fsdp'), may hold values from -0.046875 to 0.046875
- block_tenant_ids: int32 [16], replicated, may hold values from 0 to 15
- block_token_rows: int32 [16], replicated, may hold values from 1 to 128
- tenant_storage_slot: int32 [16], replicated, may hold values from 0 to 15, each once
Outputs:
- hidden_gradient: bfloat16 [2048, 26624], P('fsdp', 'tp')
- grad_a: float32 [16, 26624, 16], P('fsdp', 'tp')
- output_map_gradient: float32 [16, 16, 16384], P('fsdp')
Inputs may be any that keep to these rules, and one draw needn't show every extreme that they name: `tenant_storage_slot`: each slot number appears once.
All inputs are finite; a program needn't handle non-finite values.
Results may differ from a plain program's by a relative error of at most 0.0017.
Values may be sent and summed in bfloat16 or wider, within the bound.
A program may use at most 192 MiB of HBM per device.

v0:
```python
import jax
import jax.numpy as jnp
from jax import lax
from jax.sharding import PartitionSpec as P

BLOCK = 128


adapter_scale = 2.0


def local(
    hidden_activations_saved,
    output_cotangent,
    frozen_down_matrix,
    adapter_input_maps,
    adapter_output_maps,
    block_tenant_ids,
    block_token_rows,
    tenant_storage_slot,
):
    tok_dev, hid_dev = hidden_activations_saved.shape
    rows_tp, feat_dev = output_cotangent.shape
    tenants = tenant_storage_slot.shape[0]
    blocks = block_tenant_ids.shape[0]
    tokens = blocks * BLOCK
    fsdp_at = lax.axis_index("fsdp")
    tp_at = lax.axis_index("tp")
    tenant_hot = block_tenant_ids[:, None] == jnp.arange(tenants, dtype=jnp.int32)[None, :]
    current_block_slot = jnp.sum(jnp.where(tenant_hot, tenant_storage_slot[None, :], 0), axis=1)
    slot_hot = (
        current_block_slot[:, None] == jnp.arange(tenants, dtype=jnp.int32)[None, :]
    ).astype(jnp.bfloat16)
    live_rows = (jnp.arange(BLOCK, dtype=jnp.int32)[None, :] < block_token_rows[:, None]).reshape(
        tokens
    )
    live_local = lax.dynamic_slice_in_dim(live_rows, tp_at * rows_tp, rows_tp, 0)
    masked_local = jnp.where(
        live_local[:, None], output_cotangent, jnp.zeros((), output_cotangent.dtype)
    )
    output_map_columns = lax.all_to_all(
        adapter_output_maps, "fsdp", split_axis=2, concat_axis=0, tiled=True
    )
    dy_cols = lax.all_gather(masked_local, "tp", axis=0, tiled=True)
    b_sel = jnp.einsum(
        "bs,srd->brd", slot_hot, output_map_columns, preferred_element_type=jnp.float32
    ).astype(jnp.bfloat16)
    out_part = jnp.einsum(
        "uop,uqp->uoq",
        dy_cols.reshape(blocks, BLOCK, feat_dev),
        b_sel,
        preferred_element_type=jnp.float32,
    )
    output_side_sum = lax.psum(out_part.reshape(tokens, output_map_columns.shape[1]), "fsdp")
    reduced_output = (adapter_scale * output_side_sum).astype(jnp.bfloat16)
    rank = reduced_output.shape[1]
    blk_dev = tok_dev // BLOCK
    hot_mine = lax.dynamic_slice_in_dim(slot_hot, fsdp_at * blk_dev, blk_dev, 0)
    input_maps_every = lax.all_gather(adapter_input_maps, "fsdp", axis=0, tiled=True)
    a_mine = jnp.einsum(
        "bs,sfr->bfr", hot_mine, input_maps_every, preferred_element_type=jnp.float32
    ).astype(jnp.bfloat16)
    hidden_blocks = hidden_activations_saved.reshape(blk_dev, BLOCK, hid_dev)
    in_part = jnp.einsum("dju,dux->djx", hidden_blocks, a_mine, preferred_element_type=jnp.float32)
    input_side_sum = lax.psum(in_part.reshape(tok_dev, rank), "tp")
    reduced_input = (adapter_scale * input_side_sum).astype(jnp.bfloat16)
    low_in_all = lax.all_gather(reduced_input, "fsdp", axis=0, tiled=True)
    db_block = jnp.einsum(
        "cyx,cym->cxm",
        low_in_all.reshape(blocks, BLOCK, rank),
        dy_cols.reshape(blocks, BLOCK, feat_dev),
        preferred_element_type=jnp.float32,
    )
    db_slot = jnp.einsum(
        "bs,brd->srd", slot_hot.astype(jnp.float32), db_block, precision=lax.Precision.HIGHEST
    )
    output_map_gradient = lax.all_to_all(db_slot, "fsdp", split_axis=0, concat_axis=2, tiled=True)
    out_mine = lax.dynamic_slice_in_dim(reduced_output, fsdp_at * tok_dev, tok_dev, 0).reshape(
        blk_dev, BLOCK, rank
    )
    da_block = jnp.einsum(
        "bkf,bkr->bfr", hidden_blocks, out_mine, preferred_element_type=jnp.float32
    )
    tenant_terms = jnp.einsum(
        "bs,bfr->sfr", hot_mine.astype(jnp.float32), da_block, precision=lax.Precision.HIGHEST
    )
    grad_a = lax.psum_scatter(tenant_terms, "fsdp", scatter_dimension=0, tiled=True)
    frozen_gradient_part = lax.psum_scatter(
        lax.dot_general(
            dy_cols,
            frozen_down_matrix,
            (((1,), (1,)), ((), ())),
            preferred_element_type=jnp.float32,
        ),
        "fsdp",
        scatter_dimension=0,
        tiled=True,
    )
    adapter_gradient_part = jnp.einsum(
        "pvq,ptq->pvt", out_mine, a_mine, preferred_element_type=jnp.float32
    ).reshape(tok_dev, hid_dev)
    hidden_gradient = (frozen_gradient_part + adapter_gradient_part).astype(jnp.bfloat16)
    return (hidden_gradient, grad_a, output_map_gradient)


def solution(mesh):
    placed = (
        P("fsdp", "tp"),
        P("tp", "fsdp"),
        P("tp", "fsdp"),
        P("fsdp", "tp", None),
        P("fsdp", None, None),
        P(),
        P(),
        P(),
    )
    return jax.shard_map(
        local,
        mesh=mesh,
        in_specs=placed,
        out_specs=(P("fsdp", "tp"), P("fsdp", "tp", None), P("fsdp", None, None)),
        check_vma=False,
    )
```

profile of v0, /device:TPU:2, one launch (start us, length us, event | category | flops | bytes accessed | tf_op | source)
XLA Modules:
  0.0 659.5 jit_solution(14754227343809141583)
XLA Ops:
  7.2 0.8 fusion.10
  8.1 1.9 broadcast_select_fusion
  10.1 15.5 %copy.31 = bf16[1,16,16384]{1,0,2:T(2,128)(2,1)} copy(bf16[1,16,16384]{2,1,0:T(8,128)(2,1)} %param.12) | data formatting | bytes 1048576 | tf_op args[4]
  25.6 0.5 broadcast.9
  26.1 90.8 %reduce = bf16[16384,16]{1,0:T(8,128)(2,1)} reduce(bf16[16384,1,16]{2,1,0:T(2,128)(2,1)} %bitcast.61, bf16[]{:T(256)} %broadcast.9), dimensions={1}, to_apply=%bitcast.47.reduce_sub_computation | reduce | bytes 1048578
  116.9 6.5 reshape.62
  123.3 8.2 %all-to-all-start = ((bf16[16,2,8192]{2,1,0:T(2,128)(2,1)}), bf16[16,2,8192]{2,1,0:T(2,128)(2,1)S(1)}, u32[]{:S(2)}, u32[]{:S(2)}) async-start(bf16[16,2,8192]{2,1,0:T(2,128)(2,1)} %reshape.62), calls=%async_computation.1 | async-start | bytes 1048576 | tf_op jit(solution)/shard_map/all_to_all | solution.py:41
  131.7 9.7 %all-to-all-done = bf16[16,2,8192]{2,1,0:T(2,128)(2,1)S(1)} async-done(((bf16[16,2,8192]{2,1,0:T(2,128)(2,1)}), bf16[16,2,8192]{2,1,0:T(2,128)(2,1)S(1)}, u32[]{:S(2)}, u32[]{:S(2)}) %all-to-all-start) | async-done | bytes 524320 | tf_op jit(solution)/shard_map/all_to_all | solution.py:41
  141.5 9.8 %reshape.63 = bf16[16384,1,16]{2,1,0:T(2,128)(2,1)} reshape(bf16[16,2,8192]{2,1,0:T(2,128)(2,1)S(1)} %all-to-all-done) | data formatting | bytes 1048576
  151.2 14.9 %copy.32 = bf16[1,16,16384]{2,1,0:T(8,128)(2,1)S(1)} copy(bf16[1,16,16384]{1,0,2:T(2,128)(2,1)} %bitcast.62) | data formatting | bytes 1048576 | tf_op jit(solution)/shard_map/all_to_all | solution.py:41
  166.1 0.3 copy.47
  166.4 0.3 convolution_convert_fusion
  166.8 3.4 convolution_bitcast_fusion.1
  170.2 0.7 copy.59
  170.9 0.7 all-gather.5.cloned.1.call-update
  171.9 21.8 %fusion.22 = f32[2048,3328]{1,0:T(8,128)} fusion(bf16[2048,1024]{1,0:T(8,128)(2,1)} %all-gather.3.cloned.1.call-done, bf16[3328,1024]{1,0:T(8,128)(2,1)} %param.10), kind=kOutput, calls=%fused_computation.38 | convolution fusion | flops 13958643712 | bytes 38273024 | tf_op jit(solution)/shard_map/dot_general | solution.py:89
  193.8 105.9 %all-reduce.2.cloned.1.call-done = f32[2048,16]{0,1:T(8,128)} async-done(((f32[2048,16]{0,1:T(8,128)}), f32[2048,16]{0,1:T(8,128)}) %all-reduce.2.cloned.1.call-update) | async-done | bytes 131088 | tf_op jit(solution)/shard_map/psum | solution.py:54
  299.7 0.9 convolution_bitcast_fusion
  300.6 2.2 broadcast_multiply_fusion
  302.9 54.3 %all-gather.5.cloned.1.call-done = bf16[16,3328,16]{1,2,0:T(8,128)(2,1)} async-done(((bf16[1,3328,16]{1,2,0:T(8,128)(2,1)}), bf16[16,3328,16]{1,2,0:T(8,128)(2,1)}) %all-gather.5.cloned.1.call-update) | async-done | bytes 1703952 | tf_op jit(solution)/shard_map/all_gather | solution.py:59
  357.2 9.4 %fusion.1 = bf16[1,3328,16]{0,1,2:T(8,128)(2,1)} fusion(bf16[16,3328,16]{1,2,0:T(8,128)(2,1)} %all-gather.5.cloned.1.call-done, pred[16,16]{1,0:T(8,128)(4,1)S(1)} %iota_compare_fusion, s32[]{:T(128)S(6)} %select_n.21), kind=kOutput, calls=%fused_computation.3 | convolution fusion | flops 1703936 | bytes 1810948 | tf_op jit(solution)/shard_map/bs,sfr->bfr/dot_general | solution.py:60
  366.6 12.7 %copy.41 = bf16[1,3328,16]{1,2,0:T(8,128)(2,1)S(1)} copy(bf16[1,3328,16]{0,1,2:T(8,128)(2,1)} %fusion.1) | data formatting | bytes 212992 | tf_op jit(solution)/shard_map/bs,sfr->bfr/dot_general | solution.py:60
  379.6 18.8 %psum.15 = f32[128,16]{0,1:T(8,128)S(1)} all-reduce(f32[128,16]{0,1:T(8,128)S(1)} %convolution_bitcast_fusion.2), channel_id=1, replica_groups=mesh['fsdp'=16,'tp'=8] {'tp'}, use_global_device_ids=true, to_apply=%region_4.5 | all-reduce | flops 2048 | bytes 16384 | tf_op jit(solution)/shard_map/psum | solution.py:65
  398.4 21.1 %all_gather.11 = bf16[2048,16]{0,1:T(8,128)(2,1)S(1)} all-gather(bf16[128,16]{0,1:T(8,128)(2,1)S(1)} %multiply_convert_fusion), channel_id=1, replica_groups=mesh['fsdp'=16,'tp'=8] {'fsdp'}, dimensions={0}, use_global_device_ids=true | all-gather | bytes 69632 | tf_op jit(solution)/shard_map/all_gather | solution.py:67
  419.5 2.8 fusion.6
  422.3 1.3 fusion.3
  423.6 0.6 copy.38
  424.2 30.5 %all_to_all.36 = f32[16,16,1024]{2,1,0:T(8,128)S(1)} all-to-all(f32[16,16,1024]{2,1,0:T(8,128)S(1)} %copy.38), channel_id=1, replica_groups=mesh['fsdp'=16,'tp'=8] {'fsdp'}, dimensions={0} | all-to-all | bytes 2097152 | tf_op jit(solution)/shard_map/all_to_all | solution.py:77
  454.7 1.1 copy.46
  455.8 117.6 %reduce-scatter.3.cloned.1.call-done = f32[128,3328]{1,0:T(8,128)} async-done(((f32[2048,3328]{1,0:T(8,128)}), f32[128,3328]{1,0:T(8,128)}) %reduce-scatter.3.cloned.1.call-update) | async-done | bytes 1703952 | tf_op jit(solution)/shard_map/reduce_scatter | solution.py:88
  573.4 2.8 fusion
  576.2 76.8 %reduce-scatter.5.cloned.1.call-done = f32[1,3328,16]{1,2,0:T(8,128)} async-done(((f32[16,3328,16]{1,2,0:T(8,128)}), f32[1,3328,16]{1,2,0:T(8,128)}) %reduce-scatter.5.cloned.1.call-update) | async-done | bytes 213008 | tf_op jit(solution)/shard_map/reduce_scatter | solution.py:87
  (22 shorter events, 1.1 us)
Async XLA Ops:
  7.2 292.6 %copy-start = (bf16[128,3328]{1,0:T(8,128)(2,1)S(1)}, bf16[128,3328]{1,0:T(8,128)(2,1)}, u32[]{:S(2)}) copy-start(bf16[128,3328]{1,0:T(8,128)(2,1)} %param.8) | copy-start | bytes 2555908
  7.2 159.6 %all-gather.3.cloned.1.call-start = ((), (), s32[]{:S(2)}) async-start(), calls=%async_computation.4 | async-start | bytes 4718592 | tf_op jit(solution)/shard_map/all_gather | solution.py:44
  116.9 14.7 %copy-start.1 = (s32[16]{0:T(128)S(1)}, s32[16]{0:T(128)}, u32[]{:S(2)}) copy-start(s32[16]{0:T(128)} %param.15) | copy-start | bytes 196
  116.9 14.7 %copy-start.2 = (s32[16]{0:T(128)S(1)}, s32[16]{0:T(128)}, u32[]{:S(2)}) copy-start(s32[16]{0:T(128)} %param.13) | copy-start | bytes 196
  123.3 18.1 %all-to-all-start = ((bf16[16,2,8192]{2,1,0:T(2,128)(2,1)}), bf16[16,2,8192]{2,1,0:T(2,128)(2,1)S(1)}, u32[]{:S(2)}, u32[]{:S(2)}) async-start(bf16[16,2,8192]{2,1,0:T(2,128)(2,1)} %reshape.62), calls=%async_computation.1 | async-start | bytes 1048576 | tf_op jit(solution)/shard_map/all_to_all | solution.py:41
  131.5 168.2 %all-reduce.2.cloned.1.call-start = ((), (), s32[]{:S(2)}) async-start(), calls=%async_computation.6 | async-start | bytes 262144 | tf_op jit(solution)/shard_map/psum | solution.py:54
  170.9 186.3 %all-gather.5.cloned.1.call-start = ((), (), s32[]{:S(2)}) async-start(), calls=%async_computation.7 | async-start | bytes 1810432 | tf_op jit(solution)/shard_map/all_gather | solution.py:59
  171.6 401.8 %reduce-scatter.3.cloned.1.call-start = ((), (), s32[]{:S(2)}) async-start(), calls=%async_computation.5 | async-start | bytes 28966912 | tf_op jit(solution)/shard_map/reduce_scatter | solution.py:88
  193.6 459.3 %reduce-scatter.5.cloned.1.call-start = ((), (), s32[]{:S(2)}) async-start(), calls=%async_computation.8 | async-start | bytes 3620864 | tf_op jit(solution)/shard_map/reduce_scatter | solution.py:87
Sparse Core Ops, SparseCore 0:
  10.2 55.0 all-gather.2
  171.0 128.6 all-reduce.1
  302.4 54.7 all-gather.4
  362.1 211.2 reduce-scatter.2
  577.9 75.0 reduce-scatter.4
where the time goes:
time: 662 us; the launch traced here: 660 us
  waiting for transfers between devices  365 us (55%)
  other arithmetic  96 us (15%)
  blocking collectives  70.3 us (11%)
  local copies, waits for them, and re-layouts  62.6 us (9%)
  matrix products  43 us (6%)
  between operations  13.9 us (2%)
  starting transfers between devices  8.53 us (1%)
    reduce_scatter x1, waiting for transfers between devices, local(): lax.psum_scatter(lax.dot_general(dy_cols, frozen_down_matrix, (((1,), (1,...  118 us
    psum x1, waiting for transfers between devices, local(): lax.psum(out_part.reshape(tokens, output_map_columns.shape[1]), 'fsdp')  106 us
    unnamed x1, other arithmetic  90.8 us
    reduce_scatter x1, waiting for transfers between devices, local(): lax.psum_scatter(tenant_terms, 'fsdp', scatter_dimension=0, tiled=True)  76.8 us
    all_gather x1, waiting for transfers between devices, local(): lax.all_gather(adapter_input_maps, 'fsdp', axis=0, tiled=True)  54.3 us
    unnamed x11, local copies, waits for them, and re-layouts  32.6 us
    all_to_all x1, blocking collectives, local(): lax.all_to_all(db_slot, 'fsdp', split_axis=0, concat_axis=2, tiled=True)  30.5 us
    dot_general x1, matrix products, local(): lax.dot_general(dy_cols, frozen_down_matrix, (((1,), (1,)), ((), ())), pr...  21.8 us
  transfers between devices with their start and end apart: 6, of which 5 were waited for; matrix products, arithmetic and copies ran while one was open for 30% of the time, Pallas kernels for 0%

commit v1 on v0

v1 whole, which is shorter than its diff:
```python
import functools
import math

import jax
import jax.numpy as jnp
from jax import lax
from jax.experimental import pallas as pl
from jax.experimental.pallas import tpu as pltpu
from jax.sharding import PartitionSpec as P

BLOCK = 128
TILE = 256
MESH = pl.DeviceIdType.MESH
adapter_scale = 2.0
f32 = jnp.float32
bf16 = jnp.bfloat16

TOP = 32000.0
STEPS = 8.0 / math.log(2.0)


def nt(a, b):
    return lax.dot_general(a, b, (((1,), (1,)), ((), ())), preferred_element_type=f32)


def nn(a, b):
    return lax.dot_general(a, b, (((1,), (0,)), ((), ())), preferred_element_type=f32)


def level_of(peak):
    return jnp.ceil(jnp.log(jnp.maximum(peak, 1e-30)) * STEPS)


def kernel(
    ids, live, store, h_ref, g_ref, w_ref, a_ref, b_ref,
    o_h, o_a, o_b,
    w_all, dy, stage, part, acc, out_q, in_q, a_all, b_all, a_sel,
    lin_part, lin_own, lin_all, low_part, low_in_parts, slot_terms, slot_other,
    da_own, da_all, da_send, da_other, spread,
    w_sem, gs, gr, ss, sr, vs, vr,
):
    fs = lax.axis_index("fsdp")
    t = lax.axis_index("tp")
    k, c = fs // 2, fs % 2
    y, zl = t % 4, t // 4
    hid = h_ref.shape[1]
    feat = g_ref.shape[1]
    rank = a_ref.shape[0]
    tiles = hid // TILE
    chips = 8

    def across(j):
        return {"fsdp": 2 * j + c, "tp": t}

    def along(tt):
        return {"fsdp": fs, "tp": tt}

    sibling = {"fsdp": 2 * k + 1 - c, "tp": t}

    def slot(b):
        return store[ids[b]]

    def place(s):
        return (s % 2) * chips + s // 2

    def send(src, dst, s_sem, r_sem, dev):
        return pltpu.make_async_remote_copy(
            src_ref=src, dst_ref=dst, send_sem=s_sem, recv_sem=r_sem,
            device_id=dev, device_id_type=MESH,
        )

    def others(me, body):
        def step(i, _):
            body(lax.rem(me + i, chips))
            return 0

        lax.fori_loop(1, chips, step, 0)

    barrier = pltpu.get_barrier_semaphore()
    pl.semaphore_signal(barrier, inc=1, device_id=sibling, device_id_type=MESH)
    others(k, lambda j: pl.semaphore_signal(barrier, inc=1, device_id=across(j), device_id_type=MESH))
    others(t, lambda j: pl.semaphore_signal(barrier, inc=1, device_id=along(j), device_id_type=MESH))

    mine = pl.ds(pl.multiple_of(c * feat, feat), feat)
    w_here = pltpu.make_async_copy(w_ref, w_all.at[:, mine], w_sem)
    w_here.start()

    def masked(j):
        rows = lax.broadcasted_iota(jnp.int32, (BLOCK, feat), 0)
        g = g_ref[pl.ds(pl.multiple_of(j * BLOCK, BLOCK), BLOCK), :]
        return jnp.where(rows < live[2 * t + j], g, jnp.zeros((), bf16))

    dy[y, zl, :, mine] = masked(c)
    stage[...] = masked(1 - c)
    pl.semaphore_wait(barrier, 15)

    to_sib = send(stage, dy.at[y, zl, :, mine], ss.at[0], sr.at[0], sibling)
    to_sib.start()
    w_out = send(w_ref, w_all.at[:, mine], ss.at[1], sr.at[1], sibling)
    w_out.start()
    to_sib.wait_recv()

    def dy_send(y_from, z_from, n, tt):
        at = z_from * 4 + y_from
        return send(dy.at[y_from, z_from], dy.at[y_from, z_from], gs.at[0, n], gr.at[0, at], along(tt))

    y_next, y_prev, y_far = lax.rem(y + 1, 4), lax.rem(y + 3, 4), lax.rem(y + 2, 4)
    own = [dy_send(y, zl, 0, (1 - zl) * 4 + y)]
    own += [dy_send(y, zl, 1 + i, zl * 4 + yy) for i, yy in enumerate((y_next, y_prev, y_far))]
    for cp in own:
        cp.start()

    def a_copy(j):
        return send(a_ref, a_all.at[c * chips + k], gs.at[1, j], gr.at[1, k], across(j))

    def b_copy(j):
        cols = pl.ds(pl.multiple_of(j * 2 * feat, 2 * feat), 2 * feat)
        return send(b_ref.at[:, cols], b_all.at[c * chips + k], gs.at[2, j], gr.at[2, k], across(j))

    others(k, lambda j: a_copy(j).start())
    others(k, lambda j: b_copy(j).start())
    a_all[c * chips + k] = a_ref[...]
    b_all[c * chips + k] = b_ref[:, pl.ds(pl.multiple_of(k * 2 * feat, 2 * feat), 2 * feat)]

    def dy_wait(yy, zz):
        at = zz * 4 + yy
        send(dy.at[yy, zz], dy.at[yy, zz], gs.at[0, 0], gr.at[0, at], sibling).wait_recv()

    dy_wait(y, 1 - zl)
    relay = [dy_send(y, 1 - zl, 4 + i, zl * 4 + yy) for i, yy in enumerate((y_next, y_prev, y_far))]
    for cp in relay:
        cp.start()

    def q_copy(j):
        return send(out_q.at[j], in_q.at[k], gs.at[3, j], gr.at[3, k], across(j))

    def main_step(yy):
        def tile(n, peak):
            at = pl.ds(pl.multiple_of(n * TILE, TILE), TILE)
            p = nt(dy[yy].reshape(2 * BLOCK, 2 * feat), w_all[at, :])
            part[:, at] = p
            p = jnp.abs(p)
            return jnp.maximum(peak, jnp.maximum(p[:, :128], p[:, 128:]))

        peak = lax.fori_loop(0, tiles, tile, jnp.zeros((2 * BLOCK, 128), f32))
        level = level_of(jnp.max(peak, axis=1, keepdims=True))
        gain = TOP * jnp.exp(level * (-1.0 / STEPS))
        for zz in range(2):
            j = zz * 4 + yy
            lo = zz * BLOCK

            @pl.when(j == k)
            def _():
                acc[...] = part[lo : lo + BLOCK, :]

            @pl.when(j != k)
            def _():
                def code(n, _):
                    at = pl.ds(pl.multiple_of(n * TILE, TILE), TILE)
                    q = jnp.round(part[lo : lo + BLOCK, at] * gain[lo : lo + BLOCK])
                    out_q[j, :, at] = q.astype(jnp.int32).astype(jnp.int16)
                    return 0

                lax.fori_loop(0, tiles, code, 0)
                marks = jnp.broadcast_to(level[lo : lo + BLOCK], (BLOCK, 128))
                out_q[j, :, hid:] = marks.astype(jnp.int32).astype(jnp.int16)
                q_copy(j).start()

    w_out.wait_recv()
    w_here.wait()
    main_step(y)

    others(k, lambda j: send(a_ref, a_all.at[c * chips + j], gs.at[1, j], gr.at[1, j], across(j)).wait_recv())
    others(k, lambda j: send(b_ref.at[:, : 2 * feat], b_all.at[c * chips + j], gs.at[2, j], gr.at[2, j], across(j)).wait_recv())
    half = pl.ds(c * chips, chips)
    a_fwd = send(a_all.at[half], a_all.at[half], ss.at[2], sr.at[2], sibling)
    b_fwd = send(b_all.at[half], b_all.at[half], ss.at[3], sr.at[3], sibling)
    a_fwd.start()
    b_fwd.start()
    a_fwd.wait_recv()
    a_sel[...] = a_all[place(slot(fs))]
    lin_part[t] = nt(a_sel[...], h_ref[...])

    def lin_copy(j):
        return send(lin_part.at[t], lin_part.at[t], gs.at[4, j], gr.at[4, t], along(j))

    others(t, lambda j: lin_copy(j).start())

    for zz in range(2):
        dy_wait(y_next, zz)
    main_step(y_next)

    others(t, lambda j: send(lin_part.at[j], lin_part.at[j], gs.at[4, j], gr.at[4, j], along(j)).wait_recv())
    total = lin_part[0]
    for j in range(1, chips):
        total = total + lin_part[j]
    lin_own[...] = (adapter_scale * total).astype(bf16)

    def lin_all_copy(j):
        return send(lin_own, lin_all.at[k], gs.at[5, j], gr.at[5, k], across(j))

    others(k, lambda j: lin_all_copy(j).start())
    lin_all[k] = lin_own[...]

    for zz in range(2):
        dy_wait(y_prev, zz)
    main_step(y_prev)
    for zz in range(2):
        dy_wait(y_far, zz)
    main_step(y_far)

    b_fwd.wait_recv()

    def low_step(j, _):
        low_part[j] = nt(b_all[place(slot(2 * j + c))], dy[j % 4, j // 4])
        return 0

    lax.fori_loop(0, chips, low_step, 0)

    def low_copy(j):
        return send(low_part.at[j], low_in_parts.at[k], gs.at[6, j], gr.at[6, k], across(j))

    others(k, lambda j: low_copy(j).start())
    low_in_parts[k] = low_part[k]

    others(k, lambda j: send(lin_own, lin_all.at[j], gs.at[5, j], gr.at[5, j], across(j)).wait_recv())
    for j in range(chips):
        at = ((j % 4) * 2 + j // 4) * BLOCK
        s = slot(2 * j + c)
        value = lin_all[j]
        for n in range(2 * chips):
            hit = (s == 2 * (n % chips) + n // chips).astype(f32).astype(bf16)
            spread[n * rank : (n + 1) * rank, at : at + BLOCK] = value * hit

    def slot_tile(n, _):
        at = pl.ds(pl.multiple_of(n * TILE, TILE), TILE)
        p = nn(spread[...], dy[:, :, :, at].reshape(chips * BLOCK, TILE))
        slot_terms[:, :, :, at] = p.reshape(2, chips, rank, TILE)
        return 0

    lax.fori_loop(0, 2 * feat // TILE, slot_tile, 0)
    slot_swap = send(slot_terms.at[1 - c], slot_other, ss.at[4], sr.at[4], sibling)
    slot_swap.start()

    others(k, lambda j: send(low_part.at[j], low_in_parts.at[j], gs.at[6, j], gr.at[6, j], across(j)).wait_recv())
    total = low_in_parts[0]
    for j in range(1, chips):
        total = total + low_in_parts[j]
    low = (adapter_scale * total).astype(bf16)
    da = nn(low, h_ref[...])
    level = level_of(jnp.max(jnp.abs(da), axis=1, keepdims=True))
    gain = TOP * jnp.exp(level * (-1.0 / STEPS))
    da_own[:, :hid] = jnp.round(da * gain).astype(jnp.int32).astype(jnp.int16)
    da_own[:, hid:] = jnp.broadcast_to(level, (rank, 128)).astype(jnp.int32).astype(jnp.int16)

    def da_copy(j):
        return send(da_own, da_all.at[k], gs.at[7, j], gr.at[7, k], across(j))

    others(k, lambda j: da_copy(j).start())
    da_all[k] = da_own[...]

    slot_swap.wait_recv()
    slot_terms[c] = slot_terms[c] + slot_other[...]

    def b_cols(j):
        return pl.ds(pl.multiple_of(j * 2 * feat, 2 * feat), 2 * feat)

    def ob_copy(j):
        return send(slot_terms.at[c, j], o_b.at[:, b_cols(k)], gs.at[8, j], gr.at[8, k], across(j))

    others(k, lambda j: ob_copy(j).start())
    o_b[:, b_cols(k)] = slot_terms[c, k]

    def add_part(j):
        send(out_q.at[j], in_q.at[j], gs.at[3, j], gr.at[3, j], across(j)).wait_recv()
        scale = jnp.exp(in_q[j, :, hid:].astype(f32) * (1.0 / STEPS)) * (1.0 / TOP)
        scale = jnp.concatenate([scale, scale], axis=1)

        def tile(n, _):
            at = pl.ds(pl.multiple_of(n * TILE, TILE), TILE)
            acc[:, at] += in_q[j, :, at].astype(f32) * scale
            return 0

        lax.fori_loop(0, tiles, tile, 0)

    others(k, add_part)
    low_rows = low.astype(f32).T.astype(bf16)

    def finish(n, _):
        at = pl.ds(pl.multiple_of(n * TILE, TILE), TILE)
        o_h[:, at] = (acc[:, at] + nn(low_rows, a_sel[:, at])).astype(bf16)
        return 0

    lax.fori_loop(0, tiles, finish, 0)

    others(k, lambda j: send(da_own, da_all.at[j], gs.at[7, j], gr.at[7, j], across(j)).wait_recv())

    def da_sum(s):
        out = jnp.zeros((rank, hid), f32)
        for j in range(chips):
            hit = (slot(2 * j + c) == s).astype(f32) * (1.0 / TOP)
            scale = jnp.exp(da_all[j, :, hid:].astype(f32) * (1.0 / STEPS))[:, :1] * hit
            out = out + da_all[j, :, :hid].astype(f32) * scale
        return out

    da_send[...] = da_sum(2 * k + 1 - c)
    da_swap = send(da_send, da_other, ss.at[5], sr.at[5], sibling)
    da_swap.start()
    o_a[...] = da_sum(2 * k + c)
    da_swap.wait_recv()
    o_a[...] += da_other[...]

    others(k, lambda j: send(slot_terms.at[c, j], o_b.at[:, b_cols(j)], gs.at[8, j], gr.at[8, j], across(j)).wait_recv())

    for cp in (to_sib, w_out, a_fwd, b_fwd, slot_swap, da_swap):
        cp.wait_send()
    for cp in own + relay:
        cp.wait_send()
    for copy in (a_copy, b_copy, q_copy, lin_all_copy, low_copy, da_copy, ob_copy):
        others(k, lambda j: copy(j).wait_send())
    others(t, lambda j: lin_copy(j).wait_send())


def local(h, g, w, a, b, ids, live, store):
    tok, hid = h.shape
    feat = g.shape[1]
    rank = a.shape[2]
    wide = b.shape[2]
    chips = 8
    a_t = jnp.swapaxes(a, 1, 2).reshape(rank, hid)
    vm = pl.BlockSpec(memory_space=pltpu.VMEM)
    sm = pl.BlockSpec(memory_space=pltpu.SMEM)
    dma = pltpu.SemaphoreType.DMA
    o_h, o_a, o_b = pl.pallas_call(
        kernel,
        out_shape=(
            jax.ShapeDtypeStruct((tok, hid), bf16),
            jax.ShapeDtypeStruct((rank, hid), f32),
            jax.ShapeDtypeStruct((rank, wide), f32),
        ),
        in_specs=[sm, sm, sm, vm, vm, pl.BlockSpec(memory_space=pl.ANY), vm, vm],
        out_specs=(vm, vm, vm),
        scratch_shapes=[
            pltpu.VMEM((hid, 2 * feat), bf16),
            pltpu.VMEM((4, 2, BLOCK, 2 * feat), bf16),
            pltpu.VMEM((BLOCK, feat), bf16),
            pltpu.VMEM((2 * BLOCK, hid), f32),
            pltpu.VMEM((BLOCK, hid), f32),
            pltpu.VMEM((chips, BLOCK, hid + 128), jnp.int16),
            pltpu.VMEM((chips, BLOCK, hid + 128), jnp.int16),
            pltpu.VMEM((2 * chips, rank, hid), bf16),
            pltpu.VMEM((2 * chips, rank, 2 * feat), bf16),
            pltpu.VMEM((rank, hid), bf16),
            pltpu.VMEM((chips, rank, BLOCK), f32),
            pltpu.VMEM((rank, BLOCK), bf16),
            pltpu.VMEM((chips, rank, BLOCK), bf16),
            pltpu.VMEM((chips, rank, BLOCK), f32),
            pltpu.VMEM((chips, rank, BLOCK), f32),
            pltpu.VMEM((2, chips, rank, 2 * feat), f32),
            pltpu.VMEM((chips, rank, 2 * feat), f32),
            pltpu.VMEM((rank, hid + 128), jnp.int16),
            pltpu.VMEM((chips, rank, hid + 128), jnp.int16),
            pltpu.VMEM((rank, hid), f32),
            pltpu.VMEM((rank, hid), f32),
            pltpu.VMEM((2 * chips * rank, chips * BLOCK), bf16),
            dma,
            dma((9, 8)),
            dma((9, 8)),
            dma((6,)),
            dma((6,)),
            dma((1,)),
            dma((1,)),
        ],
        compiler_params=pltpu.CompilerParams(
            collective_id=0, has_side_effects=True, vmem_limit_bytes=62 << 20
        ),
    )(ids, live, store, h, g, w, a_t, b.reshape(rank, wide))
    return (
        o_h,
        jnp.swapaxes(o_a.reshape(1, rank, hid), 1, 2),
        o_b.reshape(1, rank, wide),
    )


def solution(mesh):
    placed = (
        P("fsdp", "tp"),
        P("tp", "fsdp"),
        P("tp", "fsdp"),
        P("fsdp", "tp", None),
        P("fsdp", None, None),
        P(),
        P(),
        P(),
    )
    return jax.shard_map(
        local,
        mesh=mesh,
        in_specs=placed,
        out_specs=(P("fsdp", "tp"), P("fsdp", "tp", None), P("fsdp", None, None)),
        check_vma=False,
    )
```

time: 662 us -> 234 us (0.35)
  waiting for transfers between devices: 365 us -> 0 us
  Pallas kernels: 0 us -> 225 us
  other arithmetic: 96 us -> 0 us
  blocking collectives: 70.3 us -> 0 us
  local copies, waits for them, and re-layouts: 62.6 us -> 6 us
  matrix products: 43 us -> 0 us
  between operations: 13.9 us -> 0.64 us
  starting transfers between devices: 8.53 us -> 0 us
    pallas_call x0 -> x1, Pallas kernels: none -> 225 us  [local(): pl.pallas_call(kernel, out_shape=(jax.ShapeDtypeStruct((tok, hid), bf16),...]
    reduce_scatter x2 -> x0, waiting for transfers between devices: 194 us -> none  [the longest x1 118 us: local(): lax.psum_scatter(lax.dot_general(dy_cols, frozen_down_matrix, (((1,), (1,...]
    psum x1 -> x0, waiting for transfers between devices: 106 us -> none  [local(): lax.psum(out_part.reshape(tokens, output_map_columns.shape[1]), 'fsdp')]
    unnamed x1 -> x0, other arithmetic: 90.8 us -> none
    all_gather x2 -> x0, waiting for transfers between devices: 54.3 us -> none  [the longest x1 54.3 us: local(): lax.all_gather(adapter_input_maps, 'fsdp', axis=0, tiled=True)]
    dot_general x9 -> x0, matrix products: 43 us -> none  [the longest x1 21.8 us: local(): lax.dot_general(dy_cols, frozen_down_matrix, (((1,), (1,)), ((), ())), pr...]
    all_to_all x1 -> x0, blocking collectives: 30.5 us -> none  [local(): lax.all_to_all(db_slot, 'fsdp', split_axis=0, concat_axis=2, tiled=True)]
    unnamed x11 -> x3, local copies, waits for them, and re-layouts: 32.6 us -> 6 us
  transfers between devices with their start and end apart: 6 -> 0, of which waited for: 5 -> 0; matrix products, arithmetic and copies ran while one was open for 30% -> 0% of each run, Pallas kernels for 0% -> 0%
where the time goes in v1:
time: 234 us; the launch traced here: 232 us
  Pallas kernels  225 us (96%)
  local copies, waits for them, and re-layouts  6 us (3%)
    pallas_call x1, Pallas kernels, local(): pl.pallas_call(kernel, out_shape=(jax.ShapeDtypeStruct((tok, hid), bf16),...  225 us
    unnamed x3, local copies, waits for them, and re-layouts  6 us

profile of v1, /device:TPU:2, one launch (start us, length us, event | category | flops | bytes accessed | tf_op | source)
XLA Modules:
  0.0 232.0 jit_solution(17037656033896369052)
XLA Ops:
  0.6 225.3 %shard_map.103 = (bf16[128,3328]{1,0:T(8,128)(2,1)}, f32[16,3328]{1,0:T(8,128)}, f32[16,16384]{1,0:T(8,128)}) custom-call(s32[16]{0:T(128)} %ids.1, s32[16]{0:T(128)} %live.1, s32[16]{0:T(128)} %store.1, bf16[128,3328]{1,0:T(8,128)(2,1)} %h_ref.1, bf16[256,1024]{1,0:T(8,128)(2,1)} %g_ref.1, bf16[3328,1024]{1,0:T(8,128)(2,1)} %w_ref.1, ...), custom_call_target="tpu_custom_call" | custom-call | tf_op jit(solution)/shard_map/pallas_call | solution.py:334
  225.9 2.1 copy.14
  228.1 1.6 copy.15
  229.7 2.3 copy.16

commit v2 on v1

v2 whole, which is shorter than its diff:
```python
import functools
import math

import jax
import jax.numpy as jnp
from jax import lax
from jax.experimental import pallas as pl
from jax.experimental.pallas import tpu as pltpu
from jax.sharding import PartitionSpec as P

BLOCK = 128
TILE = 256
MESH = pl.DeviceIdType.MESH
adapter_scale = 2.0
f32 = jnp.float32
bf16 = jnp.bfloat16

TOP = 32000.0
STEPS = 8.0 / math.log(2.0)


def nt(a, b):
    return lax.dot_general(a, b, (((1,), (1,)), ((), ())), preferred_element_type=f32)


def nn(a, b):
    return lax.dot_general(a, b, (((1,), (0,)), ((), ())), preferred_element_type=f32)


def level_of(peak):
    return jnp.ceil(jnp.log(jnp.maximum(peak, 1e-30)) * STEPS)


def kernel(
    ids, live, store, h_ref, g_ref, w_ref, a_ref, b_ref,
    o_h, o_a, o_b,
    w_all, dy, stage, part, acc, out0, out1, out2, in0, in1, in2, a_all, b_all, a_sel,
    lin_part, lin_own, lin_all, low_part, low_in_parts, slot_terms, slot_other, slot_all,
    da_own, da_all, da_send, da_other, low_kept, spread,
    gs, gr, qs, qr, ws, wr, wl, ss, sr,
):
    fs = lax.axis_index("fsdp")
    t = lax.axis_index("tp")
    k, c = fs // 2, fs % 2
    x, zh = k // 2, k % 2
    y, zl = t % 4, t // 4
    hid = h_ref.shape[1]
    feat = g_ref.shape[1]
    rank = a_ref.shape[0]
    tiles = hid // TILE
    chips = 8
    out_q, in_q = (out0, out1, out2), (in0, in1, in2)

    widths = [ref.shape[2] - 128 for ref in in_q]
    starts = [0, widths[0], widths[0] + widths[1]]

    def across(j):
        return {"fsdp": 2 * j + c, "tp": t}

    def along(tt):
        return {"fsdp": fs, "tp": tt}

    sibling = {"fsdp": 2 * k + 1 - c, "tp": t}

    def slot(b):
        return store[ids[b]]

    def place(s):
        return (s % 2) * chips + s // 2

    def send(src, dst, s_sem, r_sem, dev):
        return pltpu.make_async_remote_copy(
            src_ref=src, dst_ref=dst, send_sem=s_sem, recv_sem=r_sem,
            device_id=dev, device_id_type=MESH,
        )

    def others(me, body):
        def step(i, _):
            body(lax.rem(me + i, chips))
            return 0

        lax.fori_loop(1, chips, step, 0)

    def loop(n, body):
        def step(i, _):
            body(i)
            return 0

        lax.fori_loop(0, n, step, 0)

    def corner(j):
        xj = j // 2
        return ((xj + 1) // 2) % 2, xj // 2, j % 2

    here = corner(k)
    beside = (2 * (x + 1 - 2 * (x % 2)) + zh, 2 * (3 - x) + zh, 2 * x + 1 - zh)
    orders = ((0, 1, 2), (1, 2, 0), (2, 0, 1))

    def apart(j, p):
        there = corner(j)
        return [(here[d] + there[d]) % 2 for d in orders[p]]

    barrier = pltpu.get_barrier_semaphore()
    pl.semaphore_signal(barrier, inc=1, device_id=sibling, device_id_type=MESH)
    others(k, lambda j: pl.semaphore_signal(barrier, inc=1, device_id=across(j), device_id_type=MESH))
    others(t, lambda j: pl.semaphore_signal(barrier, inc=1, device_id=along(j), device_id_type=MESH))

    mine = pl.ds(pl.multiple_of(c * feat, feat), feat)

    def w_rows(p):
        return pl.ds(starts[p], widths[p])

    def w_here(p):
        return pltpu.make_async_copy(w_ref.at[w_rows(p)], w_all.at[w_rows(p), mine], wl.at[p])

    def w_out(p):
        return send(w_ref.at[w_rows(p)], w_all.at[w_rows(p), mine], ws.at[p], wr.at[p], sibling)

    for p in range(3):
        w_here(p).start()

    def masked(j):
        rows = lax.broadcasted_iota(jnp.int32, (BLOCK, feat), 0)
        g = g_ref[pl.ds(pl.multiple_of(j * BLOCK, BLOCK), BLOCK), :]
        return jnp.where(rows < live[2 * t + j], g, jnp.zeros((), bf16))

    dy[y, zl, :, mine] = masked(c)
    stage[...] = masked(1 - c)
    pl.semaphore_wait(barrier, 15)

    to_sib = send(stage, dy.at[y, zl, :, mine], ss.at[0], sr.at[0], sibling)
    to_sib.start()
    for p in range(3):
        w_out(p).start()
    to_sib.wait_recv()

    y_next, y_prev, y_far = lax.rem(y + 1, 4), lax.rem(y + 3, 4), lax.rem(y + 2, 4)

    def dy_send(yy, zz, n, tt):
        return send(dy.at[yy, zz], dy.at[yy, zz], gs.at[0, n], gr.at[0, zz * 4 + yy], along(tt))

    def dy_half(yy, zz, half, tt):
        rows = pl.ds(half * (BLOCK // 2), BLOCK // 2)
        piece = dy.at[yy, zz, rows]
        return send(piece, piece, gs.at[1, half * 2 + zz], gr.at[1 + half, zz * 4 + yy], along(tt))

    def dy_wait(yy, zz):
        send(dy.at[yy, zz], dy.at[yy, zz], gs.at[0, 0], gr.at[0, zz * 4 + yy], sibling).wait_recv()

    own = [dy_send(y, zl, 0, (1 - zl) * 4 + y)]
    own += [dy_send(y, zl, 1 + i, zl * 4 + yy) for i, yy in enumerate((y_next, y_prev))]
    for cp in own:
        cp.start()

    def a_copy(j):
        return send(a_ref, a_all.at[c * chips + k], gs.at[2, j], gr.at[3, k], across(j))

    def b_copy(j):
        cols = pl.ds(pl.multiple_of(j * 2 * feat, 2 * feat), 2 * feat)
        return send(b_ref.at[:, cols], b_all.at[c * chips + k], gs.at[3, j], gr.at[4, k], across(j))

    a_all[c * chips + k] = a_ref[...]
    b_all[c * chips + k] = b_ref[:, pl.ds(pl.multiple_of(k * 2 * feat, 2 * feat), 2 * feat)]

    dy_wait(y, 1 - zl)
    relay = [dy_send(y, 1 - zl, 3 + i, zl * 4 + yy) for i, yy in enumerate((y_next, y_prev))]
    for cp in relay:
        cp.start()
    others(k, lambda j: a_copy(j).start())
    others(k, lambda j: b_copy(j).start())

    half = pl.ds(c * chips, chips)
    a_fwd = send(a_all.at[half], a_all.at[half], ss.at[1], sr.at[1], sibling)
    b_fwd = send(b_all.at[half], b_all.at[half], ss.at[2], sr.at[2], sibling)

    def y_of(s):
        return lax.rem(y + s + (s // 2) * (5 - 2 * s), 4)

    def q_send(p, j, at, d):
        return send(out_q[p].at[j], in_q[p].at[at], qs.at[p, j], qr.at[p, at], across(beside[d]))

    def q_wait(p, at):
        send(out_q[p].at[0], in_q[p].at[at], qs.at[p, 0], qr.at[p, at], sibling).wait_recv()

    def cols(p, n):
        return pl.ds(pl.multiple_of(starts[p] + n * TILE, TILE), TILE)

    def inner(n):
        return pl.ds(pl.multiple_of(n * TILE, TILE), TILE)

    def code_and_send(s, zz, p, j, at, d):
        rows = pl.ds(zz * BLOCK, BLOCK)

        def top(n, peak):
            v = jnp.abs(part[s, rows, cols(p, n)])
            return jnp.maximum(peak, jnp.maximum(v[:, :128], v[:, 128:]))

        peak = lax.fori_loop(0, widths[p] // TILE, top, jnp.zeros((BLOCK, 128), f32))
        level = level_of(jnp.max(peak, axis=1, keepdims=True))
        gain = TOP * jnp.exp(level * (-1.0 / STEPS))

        def code(n):
            q = jnp.round(part[s, rows, cols(p, n)] * gain)
            out_q[p][j, :, inner(n)] = q.astype(jnp.int32).astype(jnp.int16)

        loop(widths[p] // TILE, code)
        marks = jnp.broadcast_to(level, (BLOCK, 128))
        out_q[p][j, :, widths[p] :] = marks.astype(jnp.int32).astype(jnp.int16)
        q_send(p, j, at, d).start()

    def fold(s, zz, p, at, dst):
        q_wait(p, at)
        scale = jnp.exp(in_q[p][at, :, widths[p] :].astype(f32) * (1.0 / STEPS)) * (1.0 / TOP)
        scale = jnp.concatenate([scale, scale], axis=1)
        rows = pl.ds(zz * BLOCK, BLOCK)

        def add(n):
            v = part[s, rows, cols(p, n)] + in_q[p][at, :, inner(n)].astype(f32) * scale
            if dst is None:
                part[s, rows, cols(p, n)] = v
            else:
                dst[:, cols(p, n)] = v

        loop(widths[p] // TILE, add)

    def stage1(s):
        yy = y_of(s)
        for p in range(3):
            @pl.when(s == 0)
            def _():
                w_here(p).wait()
                w_out(p).wait_recv()

            def tile(n):
                at = cols(p, n)
                part[s, :, at] = nt(dy[yy].reshape(2 * BLOCK, 2 * feat), w_all[at, :])

            loop(widths[p] // TILE, tile)
            for zz in range(2):
                j = zz * 4 + yy
                r1, r2, r3 = apart(j, p)

                @pl.when(r1 == 1)
                def _():
                    code_and_send(s, zz, p, j, r2 * 2 + r3, orders[p][0])

    def stage2(s):
        yy = y_of(s)
        for p in range(3):
            for zz in range(2):
                j = zz * 4 + yy
                r1, r2, r3 = apart(j, p)

                @pl.when(r1 == 0)
                def _():
                    fold(s, zz, p, r2 * 2 + r3, None)

                    @pl.when(r2 == 1)
                    def _():
                        code_and_send(s, zz, p, j, 4 + r3, orders[p][1])

    def stage3(s):
        yy = y_of(s)
        for p in range(3):
            for zz in range(2):
                j = zz * 4 + yy
                r1, r2, r3 = apart(j, p)

                @pl.when(r1 + r2 == 0)
                def _():
                    fold(s, zz, p, 4 + r3, None)

                    @pl.when(r3 == 1)
                    def _():
                        code_and_send(s, zz, p, j, 6, orders[p][2])

    def stage4(s):
        yy = y_of(s)
        for p in range(3):
            for zz in range(2):
                @pl.when(zz * 4 + yy == k)
                def _():
                    fold(s, zz, p, 6, acc)

    def lin_copy(j):
        return send(lin_part.at[t], lin_part.at[t], gs.at[4, j], gr.at[5, t], along(j))

    def lin_all_copy(j):
        return send(lin_own, lin_all.at[k], gs.at[5, j], gr.at[6, k], across(j))

    def low_copy(j):
        return send(low_part.at[j], low_in_parts.at[k], gs.at[6, j], gr.at[7, k], across(j))

    def da_copy(j):
        return send(da_own, da_all.at[k], gs.at[7, j], gr.at[8, k], across(j))

    def ob_copy(j):
        return send(slot_terms.at[c, j], slot_all.at[t, k], gs.at[8, j], gr.at[9, k], across(j))

    def ob_along(tt, n, to):
        return send(slot_all.at[tt], slot_all.at[tt], gs.at[9, n], gr.at[10, tt], along(to))

    def ob_wait(tt):
        send(slot_all.at[tt], slot_all.at[tt], gs.at[9, 0], gr.at[10, tt], sibling).wait_recv()

    slot_swap = send(slot_terms.at[1 - c], slot_other, ss.at[3], sr.at[3], sibling)
    da_swap = send(da_send, da_other, ss.at[4], sr.at[4], sibling)
    ob_own = [ob_along(t, 0, (1 - zl) * 4 + y)]
    ob_own += [ob_along(t, 1 + i, zl * 4 + yy) for i, yy in enumerate((y_next, y_prev, y_far))]
    t_z = (1 - zl) * 4 + y
    ob_relay = [ob_along(t_z, 4 + i, zl * 4 + yy) for i, yy in enumerate((y_next, y_prev, y_far))]
    halves = [dy_half(y_next, zz, 0, zl * 4 + y_prev) for zz in range(2)]
    halves += [dy_half(y_prev, zz, 1, zl * 4 + y_next) for zz in range(2)]

    def take_neighbours():
        for zz in (zl, 1 - zl):
            dy_wait(y_next, zz)
            dy_half(y_next, zz, 0, zl * 4 + y_prev).start()
            dy_wait(y_prev, zz)
            dy_half(y_prev, zz, 1, zl * 4 + y_next).start()

    def take_far():
        for zz in (zl, 1 - zl):
            for side in range(2):
                dy_half(y_far, zz, side, zl * 4 + y_next).wait_recv()

    def share_adapters():
        others(k, lambda j: send(a_ref, a_all.at[c * chips + j], gs.at[2, j], gr.at[3, j], across(j)).wait_recv())
        a_fwd.start()
        others(k, lambda j: send(b_ref.at[:, : 2 * feat], b_all.at[c * chips + j], gs.at[3, j], gr.at[4, j], across(j)).wait_recv())
        b_fwd.start()

    def low_activations():
        a_fwd.wait_recv()
        a_sel[...] = a_all[place(slot(fs))]
        lin_part[t] = nt(a_sel[...], h_ref[...])
        others(t, lambda j: lin_copy(j).start())

    def share_low_activations():
        others(t, lambda j: send(lin_part.at[j], lin_part.at[j], gs.at[4, j], gr.at[5, j], along(j)).wait_recv())
        total = lin_part[0]
        for j in range(1, chips):
            total = total + lin_part[j]
        lin_own[...] = (adapter_scale * total).astype(bf16)
        others(k, lambda j: lin_all_copy(j).start())
        lin_all[k] = lin_own[...]

    def low_cotangents():
        b_fwd.wait_recv()

        def low_step(j):
            low_part[j] = nt(b_all[place(slot(2 * j + c))], dy[j % 4, j // 4])

        loop(chips, low_step)
        others(k, lambda j: low_copy(j).start())
        low_in_parts[k] = low_part[k]

    def output_map_terms():
        others(k, lambda j: send(lin_own, lin_all.at[j], gs.at[5, j], gr.at[6, j], across(j)).wait_recv())
        for j in range(chips):
            at = ((j % 4) * 2 + j // 4) * BLOCK
            s = slot(2 * j + c)
            value = lin_all[j]
            for n in range(2 * chips):
                hit = (s == 2 * (n % chips) + n // chips).astype(f32).astype(bf16)
                spread[n * rank : (n + 1) * rank, at : at + BLOCK] = value * hit
        share = slot_terms.shape[3]
        cut = pl.ds(pl.multiple_of(t * share, share), share)
        terms = nn(spread[...], dy[:, :, :, cut].reshape(chips * BLOCK, share))
        slot_terms[...] = terms.reshape(2, chips, rank, share)
        slot_swap.start()

    def output_map_sums():
        slot_swap.wait_recv()
        slot_terms[c] = slot_terms[c] + slot_other[...]
        others(k, lambda j: ob_copy(j).start())
        slot_all[t, k] = slot_terms[c, k]

    def output_map_share():
        others(k, lambda j: send(slot_terms.at[c, j], slot_all.at[t, j], gs.at[8, j], gr.at[9, j], across(j)).wait_recv())
        for cp in ob_own:
            cp.start()

    def output_map_relay():
        ob_wait(t_z)
        for cp in ob_relay:
            cp.start()

    def input_map_terms():
        others(k, lambda j: send(low_part.at[j], low_in_parts.at[j], gs.at[6, j], gr.at[7, j], across(j)).wait_recv())
        total = low_in_parts[0]
        for j in range(1, chips):
            total = total + low_in_parts[j]
        low = (adapter_scale * total).astype(bf16)
        low_kept[...] = low
        da = nn(low, h_ref[...])
        level = level_of(jnp.max(jnp.abs(da), axis=1, keepdims=True))
        gain = TOP * jnp.exp(level * (-1.0 / STEPS))
        da_own[:, :hid] = jnp.round(da * gain).astype(jnp.int32).astype(jnp.int16)
        da_own[:, hid:] = jnp.broadcast_to(level, (rank, 128)).astype(jnp.int32).astype(jnp.int16)
        others(k, lambda j: da_copy(j).start())
        da_all[k] = da_own[...]

    def da_sum(s):
        out = jnp.zeros((rank, hid), f32)
        for j in range(chips):
            hit = (slot(2 * j + c) == s).astype(f32) * (1.0 / TOP)
            scale = jnp.exp(da_all[j, :, hid:].astype(f32) * (1.0 / STEPS))[:, :1] * hit
            out = out + da_all[j, :, :hid].astype(f32) * scale
        return out

    def input_map_sums():
        others(k, lambda j: send(da_own, da_all.at[j], gs.at[7, j], gr.at[8, j], across(j)).wait_recv())
        da_send[...] = da_sum(2 * k + 1 - c)
        da_swap.start()
        o_a[...] = da_sum(2 * k + c)

    plan = (
        ((), ()),
        ((take_neighbours,), (share_adapters,)),
        ((), (low_activations,)),
        ((share_low_activations, take_far, low_cotangents), (output_map_terms,)),
        ((input_map_terms, output_map_sums), ()),
        ((output_map_share,), ()),
        ((output_map_relay, input_map_sums), ()),
    )

    def when(cond, body):
        pl.when(cond)(body)

    def step(it):
        for i, (before, _) in enumerate(plan):
            if before:
                when(it == i, lambda: [f() for f in before] and None)
        when(it < 4, lambda: stage1(it))
        for i, (_, after) in enumerate(plan):
            if after:
                when(it == i, lambda: [f() for f in after] and None)
        when((it >= 1) & (it < 5), lambda: stage2(it - 1))
        when((it >= 2) & (it < 6), lambda: stage3(it - 2))
        when(it >= 3, lambda: stage4(it - 3))

    loop(7, step)

    low_rows = low_kept[...].astype(f32).T.astype(bf16)

    def finish(n):
        at = inner(n)
        o_h[:, at] = (acc[:, at] + nn(low_rows, a_sel[:, at])).astype(bf16)

    loop(tiles, finish)

    da_swap.wait_recv()
    o_a[...] += da_other[...]

    others(t, lambda j: pl.when(j != t_z)(lambda: ob_wait(j)))
    share = slot_terms.shape[3]

    def put(i):
        tt, j = i % chips, i // chips
        o_b[:, pl.ds(pl.multiple_of(i * share, share), share)] = slot_all[tt, j]

    loop(chips * chips, put)

    for cp in (to_sib, a_fwd, b_fwd, slot_swap, da_swap, *own, *relay, *halves, *ob_own, *ob_relay):
        cp.wait_send()
    for p in range(3):
        w_out(p).wait_send()
        others(k, lambda j: q_send(p, j, 0, 0).wait_send())
    for copy in (a_copy, b_copy, lin_all_copy, low_copy, da_copy, ob_copy):
        others(k, lambda j: copy(j).wait_send())
    others(t, lambda j: lin_copy(j).wait_send())


def local(h, g, w, a, b, ids, live, store):
    tok, hid = h.shape
    feat = g.shape[1]
    rank = a.shape[2]
    wide = b.shape[2]
    chips = 8
    share = 2 * feat // chips
    third = hid // (3 * TILE) * TILE
    widths = (hid - 2 * third, third, third)
    a_t = jnp.swapaxes(a, 1, 2).reshape(rank, hid)
    vm = pl.BlockSpec(memory_space=pltpu.VMEM)
    sm = pl.BlockSpec(memory_space=pltpu.SMEM)
    dma = pltpu.SemaphoreType.DMA
    o_h, o_a, o_b = pl.pallas_call(
        kernel,
        out_shape=(
            jax.ShapeDtypeStruct((tok, hid), bf16),
            jax.ShapeDtypeStruct((rank, hid), f32),
            jax.ShapeDtypeStruct((rank, wide), f32),
        ),
        in_specs=[sm, sm, sm, vm, vm, pl.BlockSpec(memory_space=pl.ANY), vm, vm],
        out_specs=(vm, vm, vm),
        scratch_shapes=[
            pltpu.VMEM((hid, 2 * feat), bf16),
            pltpu.VMEM((4, 2, BLOCK, 2 * feat), bf16),
            pltpu.VMEM((BLOCK, feat), bf16),
            pltpu.VMEM((4, 2 * BLOCK, hid), f32),
            pltpu.VMEM((BLOCK, hid), f32),
            *[pltpu.VMEM((chips, BLOCK, w + 128), jnp.int16) for w in widths],
            *[pltpu.VMEM((chips - 1, BLOCK, w + 128), jnp.int16) for w in widths],
            pltpu.VMEM((2 * chips, rank, hid), bf16),
            pltpu.VMEM((2 * chips, rank, 2 * feat), bf16),
            pltpu.VMEM((rank, hid), bf16),
            pltpu.VMEM((chips, rank, BLOCK), f32),
            pltpu.VMEM((rank, BLOCK), bf16),
            pltpu.VMEM((chips, rank, BLOCK), bf16),
            pltpu.VMEM((chips, rank, BLOCK), f32),
            pltpu.VMEM((chips, rank, BLOCK), f32),
            pltpu.VMEM((2, chips, rank, share), f32),
            pltpu.VMEM((chips, rank, share), f32),
            pltpu.VMEM((chips, chips, rank, share), f32),
            pltpu.VMEM((rank, hid + 128), jnp.int16),
            pltpu.VMEM((chips, rank, hid + 128), jnp.int16),
            pltpu.VMEM((rank, hid), f32),
            pltpu.VMEM((rank, hid), f32),
            pltpu.VMEM((rank, BLOCK), bf16),
            pltpu.VMEM((2 * chips * rank, chips * BLOCK), bf16),
            dma((10, 8)),
            dma((11, 8)),
            dma((3, 8)),
            dma((3, 7)),
            dma((3,)),
            dma((3,)),
            dma((3,)),
            dma((5,)),
            dma((5,)),
        ],
        compiler_params=pltpu.CompilerParams(
            collective_id=0, has_side_effects=True, vmem_limit_bytes=62 << 20
        ),
    )(ids, live, store, h, g, w, a_t, b.reshape(rank, wide))
    return (
        o_h,
        jnp.swapaxes(o_a.reshape(1, rank, hid), 1, 2),
        o_b.reshape(1, rank, wide),
    )


def solution(mesh):
    placed = (
        P("fsdp", "tp"),
        P("tp", "fsdp"),
        P("tp", "fsdp"),
        P("fsdp", "tp", None),
        P("fsdp", None, None),
        P(),
        P(),
        P(),
    )
    return jax.shard_map(
        local,
        mesh=mesh,
        in_specs=placed,
        out_specs=(P("fsdp", "tp"), P("fsdp", "tp", None), P("fsdp", None, None)),
        check_vma=False,
    )
```

time: 234 us -> 138 us (0.59)
  Pallas kernels: 225 us -> 130 us
    pallas_call x1, Pallas kernels: 225 us -> 130 us  [local(): pl.pallas_call(kernel, out_shape=(jax.ShapeDtypeStruct((tok, hid), bf16),...]
where the time goes in v2:
time: 138 us; the launch traced here: 137 us
  Pallas kernels  130 us (94%)
  local copies, waits for them, and re-layouts  6 us (4%)
    pallas_call x1, Pallas kernels, local(): pl.pallas_call(kernel, out_shape=(jax.ShapeDtypeStruct((tok, hid), bf16),...  130 us
    unnamed x3, local copies, waits for them, and re-layouts  6 us

profile of v2, /device:TPU:2, one launch (start us, length us, event | category | flops | bytes accessed | tf_op | source)
XLA Modules:
  0.0 136.7 jit_solution(12549874471585338464)
XLA Ops:
  0.6 130.0 %shard_map.103 = (bf16[128,3328]{1,0:T(8,128)(2,1)}, f32[16,3328]{1,0:T(8,128)}, f32[16,16384]{1,0:T(8,128)}) custom-call(s32[16]{0:T(128)} %ids.1, s32[16]{0:T(128)} %live.1, s32[16]{0:T(128)} %store.1, bf16[128,3328]{1,0:T(8,128)(2,1)} %h_ref.1, bf16[256,1024]{1,0:T(8,128)(2,1)} %g_ref.1, bf16[3328,1024]{1,0:T(8,128)(2,1)} %w_ref.1, ...), custom_call_target="tpu_custom_call" | custom-call | tf_op jit(solution)/shard_map/pallas_call | solution.py:488
  130.7 2.1 %copy.14 = bf16[128,3328]{1,0:T(8,128)(2,1)} copy(bf16[128,3328]{1,0:T(8,128)(2,1)} %get-tuple-element.12) | data formatting | bytes 1703936
  132.8 1.6 %copy.15 = f32[1,3328,16]{1,2,0:T(8,128)} copy(f32[1,3328,16]{1,2,0:T(8,128)} %bitcast.10) | data formatting | bytes 425984
  134.4 2.3 %copy.16 = f32[1,16,16384]{2,1,0:T(8,128)} copy(f32[1,16,16384]{2,1,0:T(8,128)} %bitcast.8) | data formatting | bytes 2097152

commit v3 on v2

v3 whole, which is shorter than its diff:
```python
import functools
import math

import jax
import jax.numpy as jnp
from jax import lax
from jax.experimental import pallas as pl
from jax.experimental.pallas import tpu as pltpu
from jax.sharding import PartitionSpec as P

BLOCK = 128
TILE = 256
MESH = pl.DeviceIdType.MESH
adapter_scale = 2.0
f32 = jnp.float32
bf16 = jnp.bfloat16

TOP = 32000.0
STEPS = 8.0 / math.log(2.0)


def nt(a, b):
    return lax.dot_general(a, b, (((1,), (1,)), ((), ())), preferred_element_type=f32)


def nn(a, b):
    return lax.dot_general(a, b, (((1,), (0,)), ((), ())), preferred_element_type=f32)


def level_of(peak):
    return jnp.ceil(jnp.log(jnp.maximum(peak, 1e-30)) * STEPS)


def widths_of(hid):
    tiles = hid // TILE
    return [(tiles * (p + 1) // 6 - tiles * p // 6) * TILE for p in range(6)][::-1]


def keep(h, a, b, o_h, o_a, o_b, v_h, v_a, v_b, came, left):
    ways = ((h, v_h, o_h), (b, v_b, o_b), (a, v_a, o_a))
    into = [pltpu.make_async_copy(x, v, came.at[i]) for i, (x, v, _) in enumerate(ways)]
    out = [pltpu.make_async_copy(v, o, left.at[i]) for i, (_, v, o) in enumerate(ways)]
    for cp in into:
        cp.start()
    for first, second in zip(into, out):
        first.wait()
        second.start()
    for cp in out:
        cp.wait()


def kernel(
    ids, live, store, h_ref, g_ref, w_ref, a_ref, b_ref,
    o_h, o_a, o_b,
    w_all, dy, stage, part, out_q, in_q, out_m, in_m, h_in, g_in, a_all, b_all, a_sel,
    lin_part, lin_own, lin_block, own_terms, all_terms, low_part, low_in_parts, low_rows, eye, slot_terms, slot_other, slot_all,
    da_blocks, da_out, da_in, da_sum, a_over_out, a_over_in, b_over_out, b_over_in, low_kept,
    gs, gr, qs, qr, ms, mr, ws, wr, wl, ls, ss, sr,
):
    fs = lax.axis_index("fsdp")
    t = lax.axis_index("tp")
    k, c = fs // 2, fs % 2
    x, zh = k // 2, k % 2
    y, zl = t % 4, t // 4
    hid = h_ref.shape[1]
    feat = g_ref.shape[1]
    rank = a_ref.shape[0]
    chips = 8
    share = 2 * feat // chips

    widths = widths_of(hid)
    starts = [sum(widths[:p]) for p in range(len(widths))]

    def across(j):
        return {"fsdp": 2 * j + c, "tp": t}

    def along(tt):
        return {"fsdp": fs, "tp": tt}

    sibling = {"fsdp": 2 * k + 1 - c, "tp": t}

    def slot(b):
        return store[ids[b]]

    def send(src, dst, s_sem, r_sem, dev):
        return pltpu.make_async_remote_copy(
            src_ref=src, dst_ref=dst, send_sem=s_sem, recv_sem=r_sem,
            device_id=dev, device_id_type=MESH,
        )

    def others(me, body):
        def step(i, _):
            body(lax.rem(me + i, chips))
            return 0

        lax.fori_loop(1, chips, step, 0)

    def loop(n, body):
        def step(i, _):
            body(i)
            return 0

        lax.fori_loop(0, n, step, 0)

    def corner(j):
        xj = j // 2
        return ((xj + 1) // 2) % 2, xj // 2, j % 2

    here = corner(k)
    beside = (2 * (x + 1 - 2 * (x % 2)) + zh, 2 * (3 - x) + zh, 2 * x + 1 - zh)
    orders = ((0, 1, 2), (1, 2, 0), (2, 0, 1), (0, 2, 1), (1, 0, 2), (1, 2, 0))

    def apart(j, p):
        there = corner(j)
        return [(here[d] + there[d]) % 2 for d in orders[p]]

    mine = pl.ds(pl.multiple_of(c * feat, feat), feat)

    def b_cols(xx):
        return pl.ds(pl.multiple_of(xx * 4 * feat, 4 * feat), 4 * feat)

    load_g = pltpu.make_async_copy(g_ref, g_in, ls.at[0])
    load_h = pltpu.make_async_copy(h_ref, h_in, ls.at[1])
    load_a = pltpu.make_async_copy(a_ref, a_all.at[c, x], ls.at[2])
    load_b = pltpu.make_async_copy(b_ref.at[:, b_cols(x)], b_all.at[c, x], ls.at[3])

    load_g.start()
    corners = [lax.broadcasted_iota(jnp.int32, (BLOCK, BLOCK), d) for d in range(2)]
    eye[...] = (corners[0] == corners[1]).astype(f32)

    barrier = pltpu.get_barrier_semaphore()
    pl.semaphore_signal(barrier, inc=1, device_id=sibling, device_id_type=MESH)
    others(k, lambda j: pl.semaphore_signal(barrier, inc=1, device_id=across(j), device_id_type=MESH))
    others(t, lambda j: pl.semaphore_signal(barrier, inc=1, device_id=along(j), device_id_type=MESH))

    def w_rows(p):
        return pl.ds(starts[p], widths[p])

    def w_here(p):
        return pltpu.make_async_copy(w_ref.at[w_rows(p)], w_all.at[w_rows(p), mine], wl.at[p])

    def w_out(p):
        return send(w_ref.at[w_rows(p)], w_all.at[w_rows(p), mine], ws.at[p], wr.at[p], sibling)

    for p in range(len(widths)):
        w_here(p).start()

    for cp in (load_b, load_a, load_h):
        cp.start()
    load_g.wait()

    def masked(j):
        rows = lax.broadcasted_iota(jnp.int32, (BLOCK, feat), 0)
        g = g_in[pl.ds(pl.multiple_of(j * BLOCK, BLOCK), BLOCK), :]
        return jnp.where(rows < live[2 * t + j], g, jnp.zeros((), bf16))

    dy[y, zl, :, mine] = masked(c)
    stage[...] = masked(1 - c)
    pl.semaphore_wait(barrier, 15)

    to_sib = send(stage, dy.at[y, zl, :, mine], ss.at[0], sr.at[0], sibling)
    to_sib.start()
    for p in range(len(widths)):
        w_out(p).start()
    to_sib.wait_recv()

    y_next, y_prev, y_far = lax.rem(y + 1, 4), lax.rem(y + 3, 4), lax.rem(y + 2, 4)

    def dy_send(yy, zz, n, tt):
        return send(dy.at[yy, zz], dy.at[yy, zz], gs.at[0, n], gr.at[0, zz * 4 + yy], along(tt))

    def dy_half(yy, zz, half, tt):
        rows = pl.ds(half * (BLOCK // 2), BLOCK // 2)
        piece = dy.at[yy, zz, rows]
        return send(piece, piece, gs.at[1, half * 2 + zz], gr.at[1 + half, zz * 4 + yy], along(tt))

    def dy_wait(yy, zz):
        send(dy.at[yy, zz], dy.at[yy, zz], gs.at[0, 0], gr.at[0, zz * 4 + yy], sibling).wait_recv()

    own = [dy_send(y, zl, 0, (1 - zl) * 4 + y)]
    own += [dy_send(y, zl, 1 + i, zl * 4 + yy) for i, yy in enumerate((y_next, y_prev))]
    for cp in own:
        cp.start()

    def a_copy(xx):
        return send(a_ref, a_all.at[c, x], gs.at[2, xx], gr.at[3, x], across(2 * xx + zh))

    def b_copy(xx):
        return send(b_ref.at[:, b_cols(xx)], b_all.at[c, x], gs.at[3, xx], gr.at[4, x], across(2 * xx + zh))

    def others_x(body):
        for n in range(1, 4):
            body(lax.rem(x + n, 4))

    others_x(lambda xx: a_copy(xx).start())
    others_x(lambda xx: b_copy(xx).start())

    relay = [dy_send(y, 1 - zl, 3 + i, zl * 4 + yy) for i, yy in enumerate((y_next, y_prev))]

    def take_z():
        dy_wait(y, 1 - zl)
        for cp in relay:
            cp.start()
        take_near(zl)

    partner = across(2 * x + 1 - zh)
    a_fwd = send(a_all.at[c], a_all.at[c], ss.at[1], sr.at[1], sibling)
    b_fwd = send(b_all.at[c], b_all.at[c], ss.at[2], sr.at[2], sibling)
    a_over = send(a_over_out, a_over_in, ss.at[7], sr.at[7], partner)
    b_over = send(b_over_out, b_over_in, ss.at[8], sr.at[8], partner)

    def y_of(s):
        return lax.rem(y + s + (s // 2) * (5 - 2 * s), 4)

    def q_send(p, j, at, d):
        w = widths[p]
        return send(out_q.at[p, j, :, :w], in_q.at[p, at, :, :w], qs.at[p, j], qr.at[p, at], across(beside[d]))

    def m_send(p, j, at, d):
        return send(out_m.at[p, j], in_m.at[p, at], ms.at[p, j], mr.at[p, at], across(beside[d]))

    def cols(p, n):
        return pl.ds(pl.multiple_of(starts[p] + n * TILE, TILE), TILE)

    def inner(n):
        return pl.ds(pl.multiple_of(n * TILE, TILE), TILE)

    def code_and_send(s, zz, p, j, at, d):
        rows = pl.ds(pl.multiple_of(zz * BLOCK, BLOCK), BLOCK)

        def top(n, peak):
            v = jnp.abs(part[s, rows, cols(p, n)])
            return jnp.maximum(peak, jnp.maximum(v[:, :128], v[:, 128:]))

        peak = lax.fori_loop(0, widths[p] // TILE, top, jnp.zeros((BLOCK, 128), f32))
        level = level_of(jnp.max(peak, axis=1, keepdims=True))
        gain = TOP * jnp.exp(level * (-1.0 / STEPS))

        def code(n):
            q = jnp.round(part[s, rows, cols(p, n)] * gain)
            out_q[p, j, :, inner(n)] = q.astype(jnp.int32).astype(jnp.int16)

        out_m[p, j] = jnp.broadcast_to(jnp.sum(eye[...] * level, axis=0, keepdims=True), (8, BLOCK))
        m_send(p, j, at, d).start()
        loop(widths[p] // TILE, code)
        q_send(p, j, at, d).start()

    def fold(s, zz, p, at, last):
        m_send(p, 0, at, 0).wait_recv()
        level = jnp.sum(eye[...] * in_m[p, at][:1], axis=1, keepdims=True)
        scale = jnp.exp(level * (1.0 / STEPS)) * (1.0 / TOP)
        scale = jnp.broadcast_to(scale, (BLOCK, TILE))
        rows = pl.ds(pl.multiple_of(zz * BLOCK, BLOCK), BLOCK)
        q_send(p, 0, at, 0).wait_recv()

        def add(n):
            v = part[s, rows, cols(p, n)] + in_q[p, at, :, inner(n)].astype(f32) * scale
            if last:
                v = v + nn(low_rows[...], a_sel[:, cols(p, n)])
                o_h[:, cols(p, n)] = v.astype(bf16)
            else:
                part[s, rows, cols(p, n)] = v

        loop(widths[p] // TILE, add)

    def stage1(s):
        yy = y_of(s)
        for p in range(len(widths)):
            at = w_rows(p)
            part[s, :, at] = nt(dy[yy].reshape(2 * BLOCK, 2 * feat), w_all[at, :])
            for zz in range(2):
                j = zz * 4 + yy
                r1, r2, r3 = apart(j, p)

                @pl.when(r1 == 1)
                def _():
                    code_and_send(s, zz, p, j, r2 * 2 + r3, orders[p][0])

    def stage1_alone(i):
        zz = lax.rem(zl + i, 2)
        j = zz * 4 + y
        rows = pl.ds(pl.multiple_of(zz * BLOCK, BLOCK), BLOCK)

        @pl.when(i == 1)
        def _():
            take_z()

        for p in range(len(widths)):
            @pl.when(i == 0)
            def _():
                w_here(p).wait()
                w_out(p).wait_recv()

            at = w_rows(p)
            part[0, rows, at] = nt(dy[y, zz], w_all[at, :])
            r1, r2, r3 = apart(j, p)

            @pl.when(r1 == 1)
            def _():
                code_and_send(0, zz, p, j, r2 * 2 + r3, orders[p][0])

    def stage2(s):
        yy = y_of(s)
        for p in range(len(widths)):
            for zz in range(2):
                j = zz * 4 + yy
                r1, r2, r3 = apart(j, p)

                @pl.when(r1 == 0)
                def _():
                    fold(s, zz, p, r2 * 2 + r3, False)

                    @pl.when(r2 == 1)
                    def _():
                        code_and_send(s, zz, p, j, 4 + r3, orders[p][1])

    def stage3(s):
        yy = y_of(s)
        for p in range(len(widths)):
            for zz in range(2):
                j = zz * 4 + yy
                r1, r2, r3 = apart(j, p)

                @pl.when(r1 + r2 == 0)
                def _():
                    fold(s, zz, p, 4 + r3, False)

                    @pl.when(r3 == 1)
                    def _():
                        code_and_send(s, zz, p, j, 6, orders[p][2])

    def stage4(s):
        yy = y_of(s)
        for p in range(len(widths)):
            for zz in range(2):
                @pl.when(zz * 4 + yy == k)
                def _():
                    fold(s, zz, p, 6, True)

    def lin_copy(j):
        return send(lin_part.at[t], lin_part.at[t], gs.at[4, j], gr.at[5, t], along(j))

    def lin_block_copy(j):
        return send(lin_own, lin_block, gs.at[5, j], sr.at[6], across(j))

    low_out_copy = send(low_part, low_in_parts.at[k], ss.at[5], gr.at[7, k], across(t))

    def low_copy(tt):
        return send(low_kept, low_kept, gs.at[6, tt], sr.at[5], along(tt))

    def da_copy(xx):
        return send(da_out.at[xx], da_in.at[x], gs.at[7, xx], gr.at[8, x], across(2 * xx + zh))

    da_sib = send(da_blocks.at[0], da_blocks.at[1], ss.at[4], sr.at[4], sibling)
    da_over = send(da_blocks.at[0], da_blocks.at[2], ss.at[9], sr.at[9], partner)
    da_sib_over = send(da_blocks.at[2], da_blocks.at[3], ss.at[10], sr.at[10], sibling)

    def ob_copy(j):
        return send(slot_terms.at[c, j], slot_all.at[t, k], gs.at[8, j], gr.at[9, k], across(j))

    def ob_along(tt, n, to):
        return send(slot_all.at[tt], slot_all.at[tt], gs.at[9, n], gr.at[10, tt], along(to))

    def ob_wait(tt):
        send(slot_all.at[tt], slot_all.at[tt], gs.at[9, 0], gr.at[10, tt], sibling).wait_recv()

    slot_swap = send(slot_terms.at[1 - c], slot_other, ss.at[3], sr.at[3], sibling)
    ob_own = [ob_along(t, 0, (1 - zl) * 4 + y)]
    ob_own += [ob_along(t, 1 + i, zl * 4 + yy) for i, yy in enumerate((y_next, y_prev, y_far))]
    t_z = (1 - zl) * 4 + y
    ob_relay = [ob_along(t_z, 4 + i, zl * 4 + yy) for i, yy in enumerate((y_next, y_prev, y_far))]
    halves = [dy_half(y_next, zz, 0, zl * 4 + y_prev) for zz in range(2)]
    halves += [dy_half(y_prev, zz, 1, zl * 4 + y_next) for zz in range(2)]

    def take_near(zz):
        dy_wait(y_next, zz)
        dy_half(y_next, zz, 0, zl * 4 + y_prev).start()
        dy_wait(y_prev, zz)
        dy_half(y_prev, zz, 1, zl * 4 + y_next).start()

    def take_near_second():
        take_near(1 - zl)

    def take_far():
        for zz in (zl, 1 - zl):
            for side in range(2):
                dy_half(y_far, zz, side, zl * 4 + y_next).wait_recv()

    def share_adapters():
        others_x(lambda xx: send(a_ref, a_all.at[c, xx], gs.at[2, xx], gr.at[3, xx], sibling).wait_recv())
        load_a.wait()
        a_fwd.start()
        others_x(lambda xx: send(b_ref.at[:, b_cols(0)], b_all.at[c, xx], gs.at[3, xx], gr.at[4, xx], sibling).wait_recv())
        load_b.wait()
        b_fwd.start()

    def features(z):
        return pl.ds(pl.multiple_of(z * 2 * feat, 2 * feat), 2 * feat)

    def hand_over():
        a_fwd.wait_recv()
        s = slot(2 * (2 * x + 1 - zh) + c)
        a_over_out[...] = a_all[s % 2, s // 4]
        a_over.start()
        b_fwd.wait_recv()
        s = slot(2 * t + c)
        b_over_out[...] = b_all[s % 2, s // 4, :, features(1 - zh)]
        b_over.start()

    def low_activations():
        s = slot(fs)
        a_over.wait_recv()
        here_too = ((s // 2) % 2 == zh).astype(f32).astype(bf16)
        there = ((s // 2) % 2 != zh).astype(f32).astype(bf16)
        a_sel[...] = a_all[s % 2, s // 4] * here_too + a_over_in[...] * there
        load_h.wait()
        lin_part[t] = nt(a_sel[...], h_in[...])
        others(t, lambda j: lin_copy(j).start())

    def share_low_activations():
        others(t, lambda j: send(lin_part.at[j], lin_part.at[j], gs.at[4, j], gr.at[5, j], along(j)).wait_recv())
        total = lin_part[0]
        for j in range(1, chips):
            total = total + lin_part[j]
        lin_own[...] = (adapter_scale * total).astype(bf16)

        @pl.when(k == t)
        def _():
            others(k, lambda j: lin_block_copy(j).start())

    def low_cotangents():
        s = slot(2 * t + c)
        b_over.wait_recv()
        here_too = ((s // 2) % 2 == zh).astype(f32).astype(bf16)
        there = ((s // 2) % 2 != zh).astype(f32).astype(bf16)
        b_sel = b_all[s % 2, s // 4, :, features(zh)] * here_too + b_over_in[...] * there
        low_part[...] = nt(b_sel, dy[y, zl])

        @pl.when(k != t)
        def _():
            low_out_copy.start()

    def low_sum():
        @pl.when(k == t)
        def _():
            low_in_parts[k] = low_part[...]
            others(k, lambda j: send(low_part, low_in_parts.at[j], ss.at[5], gr.at[7, j], across(j)).wait_recv())
            total = low_in_parts[0]
            for j in range(1, chips):
                total = total + low_in_parts[j]
            low_kept[...] = (adapter_scale * total).astype(bf16)
            others(t, lambda j: low_copy(j).start())

    def output_map_terms():
        @pl.when(k != t)
        def _():
            send(lin_own, lin_block, ss.at[6], sr.at[6], across(t)).wait_recv()

        @pl.when(k == t)
        def _():
            lin_block[...] = lin_own[...]

        for n in range(chips):
            own_terms[n] = nn(lin_block[...], dy[y, zl, :, n * share : (n + 1) * share])
        others(t, lambda j: terms_copy(j).start())
        all_terms[t] = own_terms[t]

    def terms_copy(j):
        return send(own_terms.at[j], all_terms.at[t], gs.at[10, j], gr.at[6, t], along(j))

    def output_map_slots():
        others(t, lambda j: send(own_terms.at[j], all_terms.at[j], gs.at[10, j], gr.at[6, j], along(j)).wait_recv())
        slots = [slot(2 * j + c) for j in range(chips)]

        def one(n):
            s = 2 * lax.rem(n, chips) + n // chips
            out = jnp.zeros((rank, share), f32)
            for j in range(chips):
                out = out + all_terms[j] * (slots[j] == s).astype(f32)
            slot_terms[n // chips, lax.rem(n, chips)] = out

        loop(2 * chips, one)
        slot_swap.start()

    def output_map_sums():
        slot_swap.wait_recv()
        slot_terms[c] = slot_terms[c] + slot_other[...]
        others(k, lambda j: ob_copy(j).start())
        slot_all[t, k] = slot_terms[c, k]

    def output_map_share():
        others(k, lambda j: send(slot_terms.at[c, j], slot_all.at[t, j], gs.at[8, j], gr.at[9, j], across(j)).wait_recv())
        for cp in ob_own:
            cp.start()

    def output_map_relay():
        ob_wait(t_z)
        for cp in ob_relay:
            cp.start()

    def input_map_terms():
        @pl.when(k != t)
        def _():
            low_copy(k).wait_recv()

        low = low_kept[...]
        low_rows[...] = low.astype(f32).T.astype(bf16)
        da_code(nn(low, h_in[...]), da_blocks.at[0])
        da_sib.start()
        da_over.start()

    def da_code(v, ref):
        level = level_of(jnp.max(jnp.abs(v), axis=1, keepdims=True))
        gain = TOP * jnp.exp(level * (-1.0 / STEPS))
        ref[:, :hid] = jnp.round(v * gain).astype(jnp.int32).astype(jnp.int16)
        ref[:, hid:] = jnp.broadcast_to(level, (rank, 128)).astype(jnp.int32).astype(jnp.int16)

    def da_value(ref, gain):
        scale = jnp.exp(ref[:, hid:].astype(f32) * (1.0 / STEPS))[:, :1] * (gain * (1.0 / TOP))
        return ref[:, :hid].astype(f32) * scale

    def input_map_pass():
        da_over.wait_recv()
        da_sib_over.start()

    def input_map_sums():
        da_sib.wait_recv()
        da_sib_over.wait_recv()
        k_z = 2 * x + 1 - zh
        slots = [slot(b) for b in (fs, 2 * k + 1 - c, 2 * k_z + c, 2 * k_z + 1 - c)]

        def one(n):
            xx = lax.rem(x + n, 4)
            out = jnp.zeros((rank, hid), f32)
            for i in range(4):
                out = out + da_value(da_blocks.at[i], (slots[i] == 2 * (2 * xx + zh) + c).astype(f32))

            @pl.when(n == 0)
            def _():
                da_sum[...] = out

            @pl.when(n > 0)
            def _():
                da_code(out, da_out.at[xx])
                da_copy(xx).start()

        loop(4, one)

    def input_map_end():
        def one(n):
            xx = lax.rem(x + n, 4)
            send(da_out.at[xx], da_in.at[xx], gs.at[7, xx], gr.at[8, xx], sibling).wait_recv()
            da_sum[...] += da_value(da_in.at[xx], 1.0)
            return 0

        lax.fori_loop(1, 4, lambda n, _: one(n), 0)
        o_a[...] = da_sum[...]

    plan = {
        1: ((share_adapters, hand_over, take_near_second, low_activations, low_cotangents), (share_low_activations, low_sum), (), ()),
        2: ((), (output_map_terms, input_map_terms), (), (output_map_slots, input_map_pass)),
        3: ((take_far,), (output_map_sums, input_map_sums), (), (output_map_share,)),
        4: ((), (), (output_map_relay,), ()),
    }

    def when(cond, body):
        pl.when(cond)(body)

    def run(it, place):
        for i, spots in plan.items():
            if spots[place]:
                when(it == i, lambda: [f() for f in spots[place]] and None)

    def step(i):
        it = i + 1
        run(it, 0)
        when(it < 4, lambda: stage1(it))
        run(it, 1)
        when(it < 5, lambda: stage2(it - 1))
        run(it, 2)
        when((it >= 2) & (it < 6), lambda: stage3(it - 2))
        when(it >= 3, lambda: stage4(it - 3))
        run(it, 3)

    loop(2, stage1_alone)
    loop(6, step)

    input_map_end()
    others(t, lambda j: pl.when(j != t_z)(lambda: ob_wait(j)))

    def put(i):
        tt, j = i % chips, i // chips
        o_b[:, pl.ds(pl.multiple_of(i * share, share), share)] = slot_all[tt, j]

    loop(chips * chips, put)

    for cp in (to_sib, a_fwd, b_fwd, a_over, b_over, slot_swap, da_sib, da_over, da_sib_over, *own, *relay, *halves, *ob_own, *ob_relay):
        cp.wait_send()
    for p in range(len(widths)):
        w_out(p).wait_send()
        others(k, lambda j: m_send(p, j, 0, 0).wait_send())
        others(k, lambda j: q_send(p, j, 0, 0).wait_send())
    for copy in (a_copy, b_copy, da_copy):
        others_x(lambda xx: copy(xx).wait_send())
    others(k, lambda j: ob_copy(j).wait_send())
    others(t, lambda j: lin_copy(j).wait_send())
    others(t, lambda j: terms_copy(j).wait_send())

    @pl.when(k == t)
    def _():
        others(t, lambda j: low_copy(j).wait_send())
        others(k, lambda j: lin_block_copy(j).wait_send())

    @pl.when(k != t)
    def _():
        low_out_copy.wait_send()


def local(h, g, w, a, b, ids, live, store):
    tok, hid = h.shape
    feat = g.shape[1]
    rank = a.shape[2]
    wide = b.shape[2]
    chips = 8
    share = 2 * feat // chips
    widths = widths_of(hid)
    a_t = jnp.swapaxes(a, 1, 2).reshape(rank, hid)
    vm = pl.BlockSpec(memory_space=pltpu.VMEM)
    sm = pl.BlockSpec(memory_space=pltpu.SMEM)
    far = pl.BlockSpec(memory_space=pl.ANY)
    dma = pltpu.SemaphoreType.DMA
    o_h, o_a, o_b = pl.pallas_call(
        kernel,
        out_shape=(
            jax.ShapeDtypeStruct((tok, hid), bf16),
            jax.ShapeDtypeStruct((rank, hid), f32),
            jax.ShapeDtypeStruct((rank, wide), f32),
        ),
        in_specs=[sm, sm, sm] + [far] * 5,
        out_specs=(vm, vm, vm),
        scratch_shapes=[
            pltpu.VMEM((hid, 2 * feat), bf16),
            pltpu.VMEM((4, 2, BLOCK, 2 * feat), bf16),
            pltpu.VMEM((BLOCK, feat), bf16),
            pltpu.VMEM((4, 2 * BLOCK, hid), f32),
            pltpu.VMEM((6, chips, BLOCK, max(widths)), jnp.int16),
            pltpu.VMEM((6, chips - 1, BLOCK, max(widths)), jnp.int16),
            pltpu.VMEM((6, chips, 8, BLOCK), f32),
            pltpu.VMEM((6, chips - 1, 8, BLOCK), f32),
            pltpu.VMEM((BLOCK, hid), bf16),
            pltpu.VMEM((2 * BLOCK, feat), bf16),
            pltpu.VMEM((2, 4, rank, hid), bf16),
            pltpu.VMEM((2, 4, rank, 4 * feat), bf16),
            pltpu.VMEM((rank, hid), bf16),
            pltpu.VMEM((chips, rank, BLOCK), f32),
            pltpu.VMEM((rank, BLOCK), bf16),
            pltpu.VMEM((rank, BLOCK), bf16),
            pltpu.VMEM((chips, rank, share), f32),
            pltpu.VMEM((chips, rank, share), f32),
            pltpu.VMEM((rank, BLOCK), f32),
            pltpu.VMEM((chips, rank, BLOCK), f32),
            pltpu.VMEM((BLOCK, rank), bf16),
            pltpu.VMEM((BLOCK, BLOCK), f32),
            pltpu.VMEM((2, chips, rank, share), f32),
            pltpu.VMEM((chips, rank, share), f32),
            pltpu.VMEM((chips, chips, rank, share), f32),
            pltpu.VMEM((4, rank, hid + 128), jnp.int16),
            pltpu.VMEM((4, rank, hid + 128), jnp.int16),
            pltpu.VMEM((4, rank, hid + 128), jnp.int16),
            pltpu.VMEM((rank, hid), f32),
            pltpu.VMEM((rank, hid), bf16),
            pltpu.VMEM((rank, hid), bf16),
            pltpu.VMEM((rank, 2 * feat), bf16),
            pltpu.VMEM((rank, 2 * feat), bf16),
            pltpu.VMEM((rank, BLOCK), bf16),
            dma((11, 8)),
            dma((11, 8)),
            dma((6, 8)),
            dma((6, 7)),
            dma((6, 8)),
            dma((6, 7)),
            dma((6,)),
            dma((6,)),
            dma((6,)),
            dma((4,)),
            dma((11,)),
            dma((11,)),
        ],
        compiler_params=pltpu.CompilerParams(
            collective_id=0, has_side_effects=True, vmem_limit_bytes=62 << 20
        ),
    )(ids, live, store, h, g, w, a_t, b.reshape(rank, wide))
    o_h, o_a, o_b = pl.pallas_call(
        keep,
        out_shape=tuple(jax.ShapeDtypeStruct(o.shape, o.dtype) for o in (o_h, o_a, o_b)),
        in_specs=[far] * 3,
        out_specs=(far,) * 3,
        scratch_shapes=[pltpu.VMEM(o.shape, o.dtype) for o in (o_h, o_a, o_b)] + [dma((3,)), dma((3,))],
        compiler_params=pltpu.CompilerParams(vmem_limit_bytes=62 << 20),
    )(o_h, o_a, o_b)
    return (
        o_h,
        jnp.swapaxes(o_a.reshape(1, rank, hid), 1, 2),
        o_b.reshape(1, rank, wide),
    )


def solution(mesh):
    placed = (
        P("fsdp", "tp"),
        P("tp", "fsdp"),
        P("tp", "fsdp"),
        P("fsdp", "tp", None),
        P("fsdp", None, None),
        P(),
        P(),
        P(),
    )
    return jax.shard_map(
        local,
        mesh=mesh,
        in_specs=placed,
        out_specs=(P("fsdp", "tp"), P("fsdp", "tp", None), P("fsdp", None, None)),
        check_vma=False,
    )
```

time: 138 us -> 117 us (0.85)
  Pallas kernels: 130 us -> 116 us
  local copies, waits for them, and re-layouts: 6 us -> 0 us
    pallas_call x1, Pallas kernels: 130 us -> 113 us  [local(): pl.pallas_call(kernel, out_shape=(jax.ShapeDtypeStruct((tok, hid), bf16),...]
    unnamed x3 -> x0, local copies, waits for them, and re-layouts: 6 us -> none
    pallas_call x0 -> x1, Pallas kernels: none -> 2.56 us  [local(): pl.pallas_call(keep, out_shape=tuple((jax.ShapeDtypeStruct(o.shape, o.dty...]
where the time goes in v3:
time: 117 us
  Pallas kernels  116 us (99%)
    pallas_call x1, Pallas kernels, local(): pl.pallas_call(kernel, out_shape=(jax.ShapeDtypeStruct((tok, hid), bf16),...  113 us
    pallas_call x1, Pallas kernels, local(): pl.pallas_call(keep, out_shape=tuple((jax.ShapeDtypeStruct(o.shape, o.dty...  2.56 us

profile of v3, /device:TPU:2, one launch (start us, length us, event | category | flops | bytes accessed | tf_op | source)
XLA Modules:
  0.0 116.7 jit_solution(14344429788109131649)
XLA Ops:
  0.6 113.3 %shard_map.103 = (bf16[128,3328]{1,0:T(8,128)(2,1)}, f32[16,3328]{1,0:T(8,128)}, f32[16,16384]{1,0:T(8,128)}) custom-call(s32[16]{0:T(128)} %ids.1, s32[16]{0:T(128)} %live.1, s32[16]{0:T(128)} %store.1, bf16[128,3328]{1,0:T(8,128)(2,1)} %h_ref.1, bf16[256,1024]{1,0:T(8,128)(2,1)} %g_ref.1, bf16[3328,1024]{1,0:T(8,128)(2,1)} %w_ref.1, ...), custom_call_target="tpu_custom_call" | custom-call | tf_op jit(solution)/shard_map/pallas_call | solution.py:632
  114.0 2.6 %shard_map.104 = (bf16[128,3328]{1,0:T(8,128)(2,1)}, f32[16,3328]{1,0:T(8,128)}, f32[16,16384]{1,0:T(8,128)}) custom-call(bf16[128,3328]{1,0:T(8,128)(2,1)} %get-tuple-element.9.h, f32[16,3328]{1,0:T(8,128)} %get-tuple-element.10.a, f32[16,16384]{1,0:T(8,128)} %get-tuple-element.11.b), custom_call_target="tpu_custom_call" | custom-call | tf_op jit(solution)/shard_map/pallas_call | solution.py:693

commit v4 on v3

--- a/solution.py
+++ b/solution.py
@@ -52,10 +52,10 @@
 def kernel(
     ids, live, store, h_ref, g_ref, w_ref, a_ref, b_ref,
     o_h, o_a, o_b,
-    w_all, dy, stage, part, out_q, in_q, out_m, in_m, h_in, g_in, a_all, b_all, a_sel,
+    w_all, dy, stage, part, out_q, in_q, h_in, g_in, a_all, b_all, a_sel,
     lin_part, lin_own, lin_block, own_terms, all_terms, low_part, low_in_parts, low_rows, eye, slot_terms, slot_other, slot_all,
     da_blocks, da_out, da_in, da_sum, a_over_out, a_over_in, b_over_out, b_over_in, low_kept,
-    gs, gr, qs, qr, ms, mr, ws, wr, wl, ls, ss, sr,
+    gs, gr, qs, qr, ws, wr, wl, ls, ss, sr,
 ):
     fs = lax.axis_index("fsdp")
     t = lax.axis_index("tp")
@@ -212,12 +212,12 @@
     def y_of(s):
         return lax.rem(y + s + (s // 2) * (5 - 2 * s), 4)
 
+    def pieces(p):
+        return 8 * widths[p] // 128
+
     def q_send(p, j, at, d):
-        w = widths[p]
-        return send(out_q.at[p, j, :, :w], in_q.at[p, at, :, :w], qs.at[p, j], qr.at[p, at], across(beside[d]))
-
-    def m_send(p, j, at, d):
-        return send(out_m.at[p, j], in_m.at[p, at], ms.at[p, j], mr.at[p, at], across(beside[d]))
+        run = pl.ds(0, pieces(p) + 1)
+        return send(out_q.at[p, j, run], in_q.at[p, at, run], qs.at[p, j], qr.at[p, at], across(beside[d]))
 
     def cols(p, n):
         return pl.ds(pl.multiple_of(starts[p] + n * TILE, TILE), TILE)
@@ -236,25 +236,26 @@
         level = level_of(jnp.max(peak, axis=1, keepdims=True))
         gain = TOP * jnp.exp(level * (-1.0 / STEPS))
 
+        marks = jnp.sum(eye[...] * level, axis=0, keepdims=True)
+        out_q[p, j, pieces(p)] = jnp.broadcast_to(marks, (16, BLOCK)).astype(jnp.int32).astype(jnp.int16)
+
         def code(n):
-            q = jnp.round(part[s, rows, cols(p, n)] * gain)
-            out_q[p, j, :, inner(n)] = q.astype(jnp.int32).astype(jnp.int16)
-
-        out_m[p, j] = jnp.broadcast_to(jnp.sum(eye[...] * level, axis=0, keepdims=True), (8, BLOCK))
-        m_send(p, j, at, d).start()
+            q = jnp.round(part[s, rows, cols(p, n)] * gain).astype(jnp.int32).astype(jnp.int16)
+            for i in range(TILE // 128):
+                out_q[p, j, pl.ds(n * 16 + 8 * i, 8)] = q[:, 128 * i : 128 * i + 128].reshape(8, 16, 128)
+
         loop(widths[p] // TILE, code)
         q_send(p, j, at, d).start()
 
     def fold(s, zz, p, at, last):
-        m_send(p, 0, at, 0).wait_recv()
-        level = jnp.sum(eye[...] * in_m[p, at][:1], axis=1, keepdims=True)
-        scale = jnp.exp(level * (1.0 / STEPS)) * (1.0 / TOP)
-        scale = jnp.broadcast_to(scale, (BLOCK, TILE))
+        q_send(p, 0, at, 0).wait_recv()
+        level = jnp.sum(eye[...] * in_q[p, at, pieces(p)].astype(f32)[:1], axis=1, keepdims=True)
+        scale = jnp.broadcast_to(jnp.exp(level * (1.0 / STEPS)) * (1.0 / TOP), (BLOCK, 128))
         rows = pl.ds(pl.multiple_of(zz * BLOCK, BLOCK), BLOCK)
-        q_send(p, 0, at, 0).wait_recv()
 
         def add(n):
-            v = part[s, rows, cols(p, n)] + in_q[p, at, :, inner(n)].astype(f32) * scale
+            q = [in_q[p, at, pl.ds(n * 16 + 8 * i, 8)].astype(f32).reshape(BLOCK, 128) for i in range(TILE // 128)]
+            v = part[s, rows, cols(p, n)] + jnp.concatenate([u * scale for u in q], axis=1)
             if last:
                 v = v + nn(low_rows[...], a_sel[:, cols(p, n)])
                 o_h[:, cols(p, n)] = v.astype(bf16)
@@ -557,9 +558,9 @@
         o_a[...] = da_sum[...]
 
     plan = {
-        1: ((share_adapters, hand_over, take_near_second, low_activations, low_cotangents), (share_low_activations, low_sum), (), ()),
+        1: ((share_adapters, hand_over, low_activations, low_cotangents, take_near_second), (share_low_activations, low_sum), (), ()),
         2: ((), (output_map_terms, input_map_terms), (), (output_map_slots, input_map_pass)),
-        3: ((take_far,), (output_map_sums, input_map_sums), (), (output_map_share,)),
+        3: ((output_map_sums, take_far), (input_map_sums,), (output_map_share,), ()),
         4: ((), (), (output_map_relay,), ()),
     }
 
@@ -598,7 +599,6 @@
         cp.wait_send()
     for p in range(len(widths)):
         w_out(p).wait_send()
-        others(k, lambda j: m_send(p, j, 0, 0).wait_send())
         others(k, lambda j: q_send(p, j, 0, 0).wait_send())
     for copy in (a_copy, b_copy, da_copy):
         others_x(lambda xx: copy(xx).wait_send())
@@ -643,10 +643,8 @@
             pltpu.VMEM((4, 2, BLOCK, 2 * feat), bf16),
             pltpu.VMEM((BLOCK, feat), bf16),
             pltpu.VMEM((4, 2 * BLOCK, hid), f32),
-            pltpu.VMEM((6, chips, BLOCK, max(widths)), jnp.int16),
-            pltpu.VMEM((6, chips - 1, BLOCK, max(widths)), jnp.int16),
-            pltpu.VMEM((6, chips, 8, BLOCK), f32),
-            pltpu.VMEM((6, chips - 1, 8, BLOCK), f32),
+            pltpu.VMEM((6, chips, max(widths) // 16 + 1, 16, 128), jnp.int16),
+            pltpu.VMEM((6, chips - 1, max(widths) // 16 + 1, 16, 128), jnp.int16),
             pltpu.VMEM((BLOCK, hid), bf16),
             pltpu.VMEM((2 * BLOCK, feat), bf16),
             pltpu.VMEM((2, 4, rank, hid), bf16),
@@ -677,8 +675,6 @@
             dma((11, 8)),
             dma((6, 8)),
             dma((6, 7)),
-            dma((6, 8)),
-            dma((6, 7)),
             dma((6,)),
             dma((6,)),
             dma((6,)),

time: 117 us -> 107 us (0.915)
  Pallas kernels: 116 us -> 105 us
    pallas_call x1, Pallas kernels: 113 us -> 103 us  [local(): pl.pallas_call(kernel, out_shape=(jax.ShapeDtypeStruct((tok, hid), bf16),...]
where the time goes in v4:
time: 107 us; the launch traced here: 106 us
  Pallas kernels  105 us (98%)
    pallas_call x1, Pallas kernels, local(): pl.pallas_call(kernel, out_shape=(jax.ShapeDtypeStruct((tok, hid), bf16),...  103 us
    pallas_call x1, Pallas kernels, local(): pl.pallas_call(keep, out_shape=tuple((jax.ShapeDtypeStruct(o.shape, o.dty...  2.56 us

profile of v4, /device:TPU:2, one launch (start us, length us, event | category | flops | bytes accessed | tf_op | source)
XLA Modules:
  0.0 106.1 jit_solution(10156208367694164362)
XLA Ops:
  0.6 102.8 %shard_map.103 = (bf16[128,3328]{1,0:T(8,128)(2,1)}, f32[16,3328]{1,0:T(8,128)}, f32[16,16384]{1,0:T(8,128)}) custom-call(s32[16]{0:T(128)} %ids.1, s32[16]{0:T(128)} %live.1, s32[16]{0:T(128)} %store.1, bf16[128,3328]{1,0:T(8,128)(2,1)} %h_ref.1, bf16[256,1024]{1,0:T(8,128)(2,1)} %g_ref.1, bf16[3328,1024]{1,0:T(8,128)(2,1)} %w_ref.1, ...), custom_call_target="tpu_custom_call" | custom-call | tf_op jit(solution)/shard_map/pallas_call | solution.py:632
  103.4 2.6 %shard_map.104 = (bf16[128,3328]{1,0:T(8,128)(2,1)}, f32[16,3328]{1,0:T(8,128)}, f32[16,16384]{1,0:T(8,128)}) custom-call(bf16[128,3328]{1,0:T(8,128)(2,1)} %get-tuple-element.9.h, f32[16,3328]{1,0:T(8,128)} %get-tuple-element.10.a, f32[16,16384]{1,0:T(8,128)} %get-tuple-element.11.b), custom_call_target="tpu_custom_call" | custom-call | tf_op jit(solution)/shard_map/pallas_call | solution.py:689

commit v5 on v4

--- a/solution.py
+++ b/solution.py
@@ -557,11 +557,21 @@
         lax.fori_loop(1, 4, lambda n, _: one(n), 0)
         o_a[...] = da_sum[...]
 
+    def output_map_end():
+        others(t, lambda j: pl.when(j != t_z)(lambda: ob_wait(j)))
+
+        def put(i):
+            tt, j = i % chips, i // chips
+            o_b[:, pl.ds(pl.multiple_of(i * share, share), share)] = slot_all[tt, j]
+
+        loop(chips * chips, put)
+
     plan = {
         1: ((share_adapters, hand_over, low_activations, low_cotangents, take_near_second), (share_low_activations, low_sum), (), ()),
         2: ((), (output_map_terms, input_map_terms), (), (output_map_slots, input_map_pass)),
-        3: ((output_map_sums, take_far), (input_map_sums,), (output_map_share,), ()),
-        4: ((), (), (output_map_relay,), ()),
+        3: ((output_map_sums, take_far), (), (output_map_share,), ()),
+        4: ((), (), (input_map_sums, output_map_relay), ()),
+        6: ((input_map_end, output_map_end), (), (), ()),
     }
 
     def when(cond, body):
@@ -585,15 +595,6 @@
 
     loop(2, stage1_alone)
     loop(6, step)
-
-    input_map_end()
-    others(t, lambda j: pl.when(j != t_z)(lambda: ob_wait(j)))
-
-    def put(i):
-        tt, j = i % chips, i // chips
-        o_b[:, pl.ds(pl.multiple_of(i * share, share), share)] = slot_all[tt, j]
-
-    loop(chips * chips, put)
 
     for cp in (to_sib, a_fwd, b_fwd, a_over, b_over, slot_swap, da_sib, da_over, da_sib_over, *own, *relay, *halves, *ob_own, *ob_relay):
         cp.wait_send()

time: 107 us -> 106 us (level)
  no operation moved by 1% of the time
where the time goes in v5:
time: 106 us
  Pallas kernels  105 us (99%)
    pallas_call x1, Pallas kernels, local(): pl.pallas_call(kernel, out_shape=(jax.ShapeDtypeStruct((tok, hid), bf16),...  102 us
    pallas_call x1, Pallas kernels, local(): pl.pallas_call(keep, out_shape=tuple((jax.ShapeDtypeStruct(o.shape, o.dty...  2.56 us

profile of v5, /device:TPU:2, one launch (start us, length us, event | category | flops | bytes accessed | tf_op | source)
XLA Modules:
  0.0 105.7 jit_solution(7103824405929310973)
XLA Ops:
  0.6 102.3 %shard_map.103 = (bf16[128,3328]{1,0:T(8,128)(2,1)}, f32[16,3328]{1,0:T(8,128)}, f32[16,16384]{1,0:T(8,128)}) custom-call(s32[16]{0:T(128)} %ids.1, s32[16]{0:T(128)} %live.1, s32[16]{0:T(128)} %store.1, bf16[128,3328]{1,0:T(8,128)(2,1)} %h_ref.1, bf16[256,1024]{1,0:T(8,128)(2,1)} %g_ref.1, bf16[3328,1024]{1,0:T(8,128)(2,1)} %w_ref.1, ...), custom_call_target="tpu_custom_call" | custom-call | tf_op jit(solution)/shard_map/pallas_call | solution.py:633
  103.0 2.6 %shard_map.104 = (bf16[128,3328]{1,0:T(8,128)(2,1)}, f32[16,3328]{1,0:T(8,128)}, f32[16,16384]{1,0:T(8,128)}) custom-call(bf16[128,3328]{1,0:T(8,128)(2,1)} %get-tuple-element.9.h, f32[16,3328]{1,0:T(8,128)} %get-tuple-element.10.a, f32[16,16384]{1,0:T(8,128)} %get-tuple-element.11.b), custom_call_target="tpu_custom_call" | custom-call | tf_op jit(solution)/shard_map/pallas_call | solution.py:690
